TPU v7x, 32 devices: a whole 2x2x4 slice. The times are simulated.
32 devices in a mesh: groups: 2 (over y), sky: 16 (over z, x, core).
Axes of the slice: x: 2, y: 2, z: 4, core: 2. Of those that a mesh axis runs over, the one named last changes fastest.
Arguments:
- wigner: bfloat16 [32, 2, 32, 64, 2048], P('sky'), may hold values from -1 to 1
- sky_blocks: bfloat16 [32, 2, 64, 2048], P('sky'), may hold values from -0.059814453 to 0.059814453
- beam: bfloat16 [2048, 8192], P('sky', 'groups'), parts along dimension 1, may hold values from -0.059814453 to 0.059814453
- block_order: int32 [32], replicated, may hold values from 0 to 31, each once
- pointing: int32 [256, 1024], P(('groups', 'sky')), parts along dimension 0, may hold values from 0 to 524287
Outputs:
- timestream: float32 [256, 1024], P(('groups', 'sky')), parts along dimension 0
There are 2 independent parts, one for each index of `groups`. A program takes and returns all parts, laid end to end along the dimension named above; an argument that names none is the same for every part. Nothing has to cross between parts.
Inputs may be any that keep to these rules, and one draw needn't show every extreme that they name: `block_order`: each of the 32 m-blocks is listed exactly once.
All inputs are finite; a program needn't handle non-finite values.
Results may differ from a plain program's by a relative error of at most 0.0048.
Values may be sent and summed in bfloat16 or wider, within the bound.
A program may use at most 320 MiB of HBM per device.

v0:
```python
import math

import jax
import jax.numpy as jnp
from jax import lax
from jax.sharding import PartitionSpec as P


def spin_phases(m_values, pixels, cycle_pixels):
    phase_index = pixels[..., None] * m_values % cycle_pixels
    angles = phase_index.astype(jnp.float32) * (2.0 * math.pi / cycle_pixels)
    weight = jnp.where(m_values == 0, 1.0, 2.0).astype(jnp.float32)
    cos_part = (weight * jnp.cos(angles)).astype(jnp.bfloat16)
    sin_part = (weight * jnp.sin(angles)).astype(jnp.bfloat16)
    return (cos_part, sin_part)


def orient_parts(cycle_re, cycle_im, orients, orient_bins):
    spin_count = cycle_re.shape[-1]
    k_values = jnp.arange(spin_count, dtype=jnp.int32)
    phase_index = orients[..., None] * k_values % orient_bins
    angles = phase_index.astype(jnp.float32) * (2.0 * math.pi / orient_bins)
    weight = jnp.where(k_values == 0, 1.0, 2.0).astype(jnp.float32)
    terms = cycle_re * jnp.cos(angles) - cycle_im * jnp.sin(angles)
    return jnp.sum(weight * terms, axis=-1)


def body(wigner, sky_blocks, beam, block_order, pointing):
    device = lax.axis_index("sky")
    blocks_here, cycle_count, spin_count, block_size, degree_count = wigner.shape
    detectors = beam.shape[1] // (2 * spin_count)
    cycle_pixels = 2 * degree_count
    orient_bins = 4 * spin_count
    pair_count = cycle_count * detectors
    m_count = blocks_here * block_size
    own_blocks = lax.dynamic_slice_in_dim(block_order, device * blocks_here, blocks_here)
    m_local = own_blocks[:, None] * block_size + jnp.arange(block_size, dtype=jnp.int32)[None, :]
    degree_index = jnp.arange(degree_count, dtype=jnp.int32)
    spin_index = jnp.arange(spin_count, dtype=jnp.int32)
    in_band = (degree_index >= m_local[:, None, None, :, None]) & (
        degree_index >= spin_index[None, None, :, None, None]
    )
    sky_values = sky_blocks.astype(jnp.float32)
    table_values = wigner.astype(jnp.float32)
    coeff_re = jnp.where(in_band, table_values * sky_values[:, 0][:, None, None], 0.0).astype(
        jnp.bfloat16
    )
    coeff_im = jnp.where(in_band, table_values * sky_values[:, 1][:, None, None], 0.0).astype(
        jnp.bfloat16
    )
    coeff_both = jnp.stack([coeff_re, coeff_im], axis=0)
    beam_piece = lax.all_gather(beam, "sky", axis=0, tiled=True)
    piece_rows = beam_piece.shape[0]
    halves = beam_piece.reshape(piece_rows, 2, detectors, spin_count)
    beam_re = halves[:, 0]
    beam_im = halves[:, 1]
    first_part = jnp.stack([beam_re, beam_im], axis=1)
    second_part = jnp.stack([-beam_im, beam_re], axis=1)
    beam_block = jnp.stack([first_part, second_part], axis=0)
    spin_sums = jnp.einsum(
        "xbrkil,xlcdk->rdckbi", coeff_both, beam_block, preferred_element_type=jnp.float32
    )
    spin_sums = spin_sums.reshape(pair_count, 2, spin_count, m_count).astype(jnp.bfloat16)
    exchanged = lax.all_to_all(spin_sums, "sky", split_axis=0, concat_axis=3, tiled=True)
    pairs_here = exchanged.shape[0]
    m_all = (
        block_order[:, None] * block_size + jnp.arange(block_size, dtype=jnp.int32)[None, :]
    ).reshape(-1)
    spin_re = exchanged[:, 0]
    spin_im = exchanged[:, 1]
    pixels = pointing // orient_bins
    orients = pointing % orient_bins
    row_block = min(512, cycle_pixels)
    block_starts = jnp.arange(cycle_pixels // row_block, dtype=jnp.int32) * row_block

    def grid_rows(first_pixel):
        cos_part, sin_part = spin_phases(
            m_all, first_pixel + jnp.arange(row_block, dtype=jnp.int32), cycle_pixels
        )
        grid_re = jnp.einsum(
            "jh,pkh->pjk", cos_part, spin_re, preferred_element_type=jnp.float32
        ) - jnp.einsum("jh,pkh->pjk", sin_part, spin_im, preferred_element_type=jnp.float32)
        grid_im = jnp.einsum(
            "jh,pkh->pjk", cos_part, spin_im, preferred_element_type=jnp.float32
        ) + jnp.einsum("jh,pkh->pjk", sin_part, spin_re, preferred_element_type=jnp.float32)
        return (grid_re, grid_im)

    grid_re, grid_im = lax.map(grid_rows, block_starts)
    grid_re = jnp.moveaxis(grid_re, 0, 1).reshape(pairs_here, cycle_pixels, spin_count)
    grid_im = jnp.moveaxis(grid_im, 0, 1).reshape(pairs_here, cycle_pixels, spin_count)

    def pick_rows(grid_table, pixel_rows):
        return grid_table[pixel_rows]

    cycle_re = jax.vmap(pick_rows)(grid_re, pixels)
    cycle_im = jax.vmap(pick_rows)(grid_im, pixels)
    timestream = orient_parts(cycle_re, cycle_im, orients, orient_bins)
    return timestream


def solution(mesh):
    return jax.shard_map(
        body,
        mesh=mesh,
        in_specs=(
            P("sky", None, None, None, None),
            P("sky", None, None, None),
            P("sky", "groups"),
            P(),
            P(("groups", "sky"), None),
        ),
        out_specs=P(("groups", "sky"), None),
        check_vma=False,
    )
```

profile of v0, /device:TPU:0, one launch (start us, length us, event | category | flops | bytes accessed | tf_op | source)
XLA Modules:
  0.0 1155.1 jit_solution(8994976267196761914)
XLA Ops:
  6.5 2.3 copy.19
  8.9 1.5 convert_element_type.43
  10.7 1.2 slice_bitcast_fusion.3
  11.9 8.5 broadcast_and_fusion
  20.5 37.8 %fusion.63 = (bf16[1,2,2,32,64,2048]{5,4,0,2,1,3:T(8,128)(2,1)}, bf16[1,2,2,32,64,2048]{5,4,0,2,1,3:T(8,128)(2,1)}) fusion(f32[2,64,2048]{2,1,0:T(8,128)S(1)} %get-tuple-element.170, pred[2,32,64,2048]{3,2,0,1:T(8,128)(4,1)} %broadcast_and_fusion, bf16[2,2,32,64,2048]{4,3,2,1,0:T(8,128)(2,1)} %param.7, f32[2,64,2048]{2,1,0:T(8,128)S(1)} %copy-done.1), kind=kLoop, calls=%fused_computation.60 | loop fusion | flops 117440512 | bytes 111149056 | tf_op jit(solution)/shard_map/stack | solution.py:51
  58.2 84.3 %all-gather.2.cloned.1.call-done = bf16[2048,4096]{0,1:T(8,128)(2,1)} async-done(((bf16[128,4096]{0,1:T(8,128)(2,1)}), bf16[2048,4096]{0,1:T(8,128)(2,1)}) %all-gather.2.cloned.1.call-update) | async-done | bytes 16777232 | tf_op jit(solution)/shard_map/all_gather | solution.py:52
  142.6 12.4 %fusion.81 = (bf16[2048,1,64,32]{0,3,2,1:T(8,128)(2,1)}, bf16[2048,1,64,32]{0,3,2,1:T(8,128)(2,1)}) fusion(bf16[2048,2,64,32]{0,3,2,1:T(8,128)(2,1)} %bitcast.137), kind=kLoop, calls=%fused_computation.107 | loop fusion | bytes 33554432 | tf_op jit(solution)/shard_map/slice | solution.py:56
  155.0 11.3 copy.33
  166.3 16.6 %copy_negate_fusion = bf16[2048,1,64,32]{0,2,1,3:T(8,128)(2,1)} fusion(bf16[2048,1,64,32]{0,3,2,1:T(8,128)(2,1)} %get-tuple-element.166), kind=kLoop, calls=%fused_computation.66 | loop fusion | flops 4194304 | bytes 16777216 | tf_op jit(solution)/shard_map/neg | solution.py:58
  182.9 20.2 %copy.22 = bf16[1,2048,2,64,32]{1,3,0,2,4:T(8,128)(2,1)} copy(bf16[1,2048,2,64,32]{1,4,3,2,0:T(8,128)(2,1)} %bitcast.138) | data formatting | bytes 33554432 | tf_op jit(solution)/shard_map/stack | solution.py:59
  203.1 6.8 maximum_bitcast_fusion.4
  210.0 40.2 %fusion.69 = bf16[2,64,2,32,2,64]{5,1,0,4,2,3:T(8,128)(2,1)S(1)} fusion(bf16[1,2,2,32,64,2048]{5,4,0,2,1,3:T(8,128)(2,1)} %get-tuple-element.165, bf16[1,2,2,32,64,2048]{5,4,0,2,1,3:T(8,128)(2,1)} %get-tuple-element.164, bf16[1,2048,2,64,32]{1,3,0,2,4:T(8,128)(2,1)} %maximum_bitcast_fusion.4, bf16[1,2048,2,64,32]{1,3,0,2,4:T(8,128)(2,1)} %copy.22), kind=kOutput, calls=%fused_computation.74 | convolution fusion | flops 8792309760 | bytes 102760448 | tf_op jit(solution)/shard_map/xbrkil,xlcdk->rdckbi/dot_general | solution.py:60
  250.1 6.3 copy.25
  256.4 7.8 convert_element_type.48
  264.2 3.7 all-to-all-start
  268.5 0.6 add_select_fusion.2
  269.2 39.8 %all-to-all-done = bf16[128,2,32,128]{3,2,1,0:T(8,128)(2,1)S(1)} async-done(((bf16[128,2,32,128]{3,2,1,0:T(8,128)(2,1)}), bf16[128,2,32,128]{3,2,1,0:T(8,128)(2,1)S(1)}, u32[]{:S(2)}, u32[]{:S(2)}) %all-to-all-start) | async-done | bytes 2097184 | tf_op jit(solution)/shard_map/all_to_all | solution.py:64
  309.7 558.3 %while.16 = (s32[]{:T(128)}, f32[8,8,512,32]{2,3,1,0:T(8,128)}, f32[8,8,512,32]{2,3,1,0:T(8,128)}, s32[8]{0:T(128)S(1)}, bf16[8,32,2048]{2,1,0:T(8,128)(2,1)S(1)...) while((s32[]{:T(128)}, f32[8,8,512,32]{2,3,1,0:T(8,128)}, ...), condition=%wide.region_1.2_spmd.clone.clone, body=%wide.region_0.1_spmd.clone.clone.sunk | while | flops 2214861312 | bytes 7458021 | solution.py:88
  310.3 0.6 dynamic_slice.15
  310.9 0.6 iota_add_fusion.6
  311.5 15.9 %fusion.108 = f32[512,8,32]{0,2,1:T(8,128)S(1)} fusion(bf16[8,32,2048]{2,1,0:T(8,128)(2,1)S(1)} %get-tuple-element.235, s32[2048]{0:T(1024)S(1)} %add.229, s32[512]{0:T(512)S(1)} %iota_add_fusion.6, f32[2048]{0:T(1024)S(1)} %compare_select_fusion.4), kind=kOutput, calls=%fused_computation.16.clone.1 | convolution fusion | flops 553648128 | bytes 1591296 | tf_op jit(solution)/shard_map/while/body/eval_jaxpr/jh,pkh->pjk/dot_general | solution.py:85
  327.5 16.9 %fusion.109 = f32[8,8,512,32]{2,3,1,0:T(8,128)} fusion(f32[8,8,512,32]{2,3,1,0:T(8,128)} %get-tuple-element.225, s32[]{:T(128)} %get-tuple-element.223, f32[512,8,32]{0,2,1:T(8,128)S(1)} %fusion.108, bf16[8,32,2048]{2,1,0:T(8,128)(2,1)S(1)} %get-tuple-element.236, s32[2048]{0:T(1024)S(1)} %add.229, s32[512]{0:T(512)S(1)} %iota_add_fusion.6, ...), kind=kOutput, calls=%fused_computation.29.clone.1 | convolution fusion | flops 553779200 | bytes 2116096 | tf_op jit(solution)/shard_map/while/body/eval_jaxpr/jh,pkh->pjk/dot_general | solution.py:83
  344.4 16.2 %fusion.106 = f32[512,8,32]{0,2,1:T(8,128)S(1)} fusion(bf16[8,32,2048]{2,1,0:T(8,128)(2,1)S(1)} %get-tuple-element.236, s32[2048]{0:T(1024)S(1)} %add.229, s32[512]{0:T(512)S(1)} %iota_add_fusion.6, f32[2048]{0:T(1024)S(1)} %compare_select_fusion.4), kind=kOutput, calls=%fused_computation.17.clone.1 | convolution fusion | flops 553648128 | bytes 1591296 | tf_op jit(solution)/shard_map/while/body/eval_jaxpr/jh,pkh->pjk/dot_general | solution.py:82
  360.5 18.6 %fusion.107 = f32[8,8,512,32]{2,3,1,0:T(8,128)} fusion(f32[8,8,512,32]{2,3,1,0:T(8,128)} %get-tuple-element.224, s32[]{:T(128)} %get-tuple-element.223, f32[512,8,32]{0,2,1:T(8,128)S(1)} %fusion.106, bf16[8,32,2048]{2,1,0:T(8,128)(2,1)S(1)} %get-tuple-element.235, s32[2048]{0:T(1024)S(1)} %add.229, s32[512]{0:T(512)S(1)} %iota_add_fusion.6, ...), kind=kOutput, calls=%fused_computation.26.clone.1 | convolution fusion | flops 553779200 | bytes 2116096 | tf_op jit(solution)/shard_map/while/body/eval_jaxpr/jh,pkh->pjk/dot_general | solution.py:80
  380.1 0.6 iota_add_fusion.6
  380.8 16.2 %fusion.108 = f32[512,8,32]{0,2,1:T(8,128)S(1)} fusion(bf16[8,32,2048]{2,1,0:T(8,128)(2,1)S(1)} %get-tuple-element.235, s32[2048]{0:T(1024)S(1)} %add.229, s32[512]{0:T(512)S(1)} %iota_add_fusion.6, f32[2048]{0:T(1024)S(1)} %compare_select_fusion.4), kind=kOutput, calls=%fused_computation.16.clone.1 | convolution fusion | flops 553648128 | bytes 1591296 | tf_op jit(solution)/shard_map/while/body/eval_jaxpr/jh,pkh->pjk/dot_general | solution.py:85
  397.0 16.9 %fusion.109 = f32[8,8,512,32]{2,3,1,0:T(8,128)} fusion(f32[8,8,512,32]{2,3,1,0:T(8,128)} %get-tuple-element.225, s32[]{:T(128)} %get-tuple-element.223, f32[512,8,32]{0,2,1:T(8,128)S(1)} %fusion.108, bf16[8,32,2048]{2,1,0:T(8,128)(2,1)S(1)} %get-tuple-element.236, s32[2048]{0:T(1024)S(1)} %add.229, s32[512]{0:T(512)S(1)} %iota_add_fusion.6, ...), kind=kOutput, calls=%fused_computation.29.clone.1 | convolution fusion | flops 553779200 | bytes 2116096 | tf_op jit(solution)/shard_map/while/body/eval_jaxpr/jh,pkh->pjk/dot_general | solution.py:83
  413.9 16.0 %fusion.106 = f32[512,8,32]{0,2,1:T(8,128)S(1)} fusion(bf16[8,32,2048]{2,1,0:T(8,128)(2,1)S(1)} %get-tuple-element.236, s32[2048]{0:T(1024)S(1)} %add.229, s32[512]{0:T(512)S(1)} %iota_add_fusion.6, f32[2048]{0:T(1024)S(1)} %compare_select_fusion.4), kind=kOutput, calls=%fused_computation.17.clone.1 | convolution fusion | flops 553648128 | bytes 1591296 | tf_op jit(solution)/shard_map/while/body/eval_jaxpr/jh,pkh->pjk/dot_general | solution.py:82
  429.8 18.8 %fusion.107 = f32[8,8,512,32]{2,3,1,0:T(8,128)} fusion(f32[8,8,512,32]{2,3,1,0:T(8,128)} %get-tuple-element.224, s32[]{:T(128)} %get-tuple-element.223, f32[512,8,32]{0,2,1:T(8,128)S(1)} %fusion.106, bf16[8,32,2048]{2,1,0:T(8,128)(2,1)S(1)} %get-tuple-element.235, s32[2048]{0:T(1024)S(1)} %add.229, s32[512]{0:T(512)S(1)} %iota_add_fusion.6, ...), kind=kOutput, calls=%fused_computation.26.clone.1 | convolution fusion | flops 553779200 | bytes 2116096 | tf_op jit(solution)/shard_map/while/body/eval_jaxpr/jh,pkh->pjk/dot_general | solution.py:80
  449.6 0.6 iota_add_fusion.6
  450.2 16.2 %fusion.108 = f32[512,8,32]{0,2,1:T(8,128)S(1)} fusion(bf16[8,32,2048]{2,1,0:T(8,128)(2,1)S(1)} %get-tuple-element.235, s32[2048]{0:T(1024)S(1)} %add.229, s32[512]{0:T(512)S(1)} %iota_add_fusion.6, f32[2048]{0:T(1024)S(1)} %compare_select_fusion.4), kind=kOutput, calls=%fused_computation.16.clone.1 | convolution fusion | flops 553648128 | bytes 1591296 | tf_op jit(solution)/shard_map/while/body/eval_jaxpr/jh,pkh->pjk/dot_general | solution.py:85
  466.4 16.8 %fusion.109 = f32[8,8,512,32]{2,3,1,0:T(8,128)} fusion(f32[8,8,512,32]{2,3,1,0:T(8,128)} %get-tuple-element.225, s32[]{:T(128)} %get-tuple-element.223, f32[512,8,32]{0,2,1:T(8,128)S(1)} %fusion.108, bf16[8,32,2048]{2,1,0:T(8,128)(2,1)S(1)} %get-tuple-element.236, s32[2048]{0:T(1024)S(1)} %add.229, s32[512]{0:T(512)S(1)} %iota_add_fusion.6, ...), kind=kOutput, calls=%fused_computation.29.clone.1 | convolution fusion | flops 553779200 | bytes 2116096 | tf_op jit(solution)/shard_map/while/body/eval_jaxpr/jh,pkh->pjk/dot_general | solution.py:83
  483.3 16.0 %fusion.106 = f32[512,8,32]{0,2,1:T(8,128)S(1)} fusion(bf16[8,32,2048]{2,1,0:T(8,128)(2,1)S(1)} %get-tuple-element.236, s32[2048]{0:T(1024)S(1)} %add.229, s32[512]{0:T(512)S(1)} %iota_add_fusion.6, f32[2048]{0:T(1024)S(1)} %compare_select_fusion.4), kind=kOutput, calls=%fused_computation.17.clone.1 | convolution fusion | flops 553648128 | bytes 1591296 | tf_op jit(solution)/shard_map/while/body/eval_jaxpr/jh,pkh->pjk/dot_general | solution.py:82
  499.2 18.8 %fusion.107 = f32[8,8,512,32]{2,3,1,0:T(8,128)} fusion(f32[8,8,512,32]{2,3,1,0:T(8,128)} %get-tuple-element.224, s32[]{:T(128)} %get-tuple-element.223, f32[512,8,32]{0,2,1:T(8,128)S(1)} %fusion.106, bf16[8,32,2048]{2,1,0:T(8,128)(2,1)S(1)} %get-tuple-element.235, s32[2048]{0:T(1024)S(1)} %add.229, s32[512]{0:T(512)S(1)} %iota_add_fusion.6, ...), kind=kOutput, calls=%fused_computation.26.clone.1 | convolution fusion | flops 553779200 | bytes 2116096 | tf_op jit(solution)/shard_map/while/body/eval_jaxpr/jh,pkh->pjk/dot_general | solution.py:80
  519.0 0.6 iota_add_fusion.6
  519.6 16.2 %fusion.108 = f32[512,8,32]{0,2,1:T(8,128)S(1)} fusion(bf16[8,32,2048]{2,1,0:T(8,128)(2,1)S(1)} %get-tuple-element.235, s32[2048]{0:T(1024)S(1)} %add.229, s32[512]{0:T(512)S(1)} %iota_add_fusion.6, f32[2048]{0:T(1024)S(1)} %compare_select_fusion.4), kind=kOutput, calls=%fused_computation.16.clone.1 | convolution fusion | flops 553648128 | bytes 1591296 | tf_op jit(solution)/shard_map/while/body/eval_jaxpr/jh,pkh->pjk/dot_general | solution.py:85
  535.8 16.9 %fusion.109 = f32[8,8,512,32]{2,3,1,0:T(8,128)} fusion(f32[8,8,512,32]{2,3,1,0:T(8,128)} %get-tuple-element.225, s32[]{:T(128)} %get-tuple-element.223, f32[512,8,32]{0,2,1:T(8,128)S(1)} %fusion.108, bf16[8,32,2048]{2,1,0:T(8,128)(2,1)S(1)} %get-tuple-element.236, s32[2048]{0:T(1024)S(1)} %add.229, s32[512]{0:T(512)S(1)} %iota_add_fusion.6, ...), kind=kOutput, calls=%fused_computation.29.clone.1 | convolution fusion | flops 553779200 | bytes 2116096 | tf_op jit(solution)/shard_map/while/body/eval_jaxpr/jh,pkh->pjk/dot_general | solution.py:83
  552.7 16.0 %fusion.106 = f32[512,8,32]{0,2,1:T(8,128)S(1)} fusion(bf16[8,32,2048]{2,1,0:T(8,128)(2,1)S(1)} %get-tuple-element.236, s32[2048]{0:T(1024)S(1)} %add.229, s32[512]{0:T(512)S(1)} %iota_add_fusion.6, f32[2048]{0:T(1024)S(1)} %compare_select_fusion.4), kind=kOutput, calls=%fused_computation.17.clone.1 | convolution fusion | flops 553648128 | bytes 1591296 | tf_op jit(solution)/shard_map/while/body/eval_jaxpr/jh,pkh->pjk/dot_general | solution.py:82
  568.7 18.8 %fusion.107 = f32[8,8,512,32]{2,3,1,0:T(8,128)} fusion(f32[8,8,512,32]{2,3,1,0:T(8,128)} %get-tuple-element.224, s32[]{:T(128)} %get-tuple-element.223, f32[512,8,32]{0,2,1:T(8,128)S(1)} %fusion.106, bf16[8,32,2048]{2,1,0:T(8,128)(2,1)S(1)} %get-tuple-element.235, s32[2048]{0:T(1024)S(1)} %add.229, s32[512]{0:T(512)S(1)} %iota_add_fusion.6, ...), kind=kOutput, calls=%fused_computation.26.clone.1 | convolution fusion | flops 553779200 | bytes 2116096 | tf_op jit(solution)/shard_map/while/body/eval_jaxpr/jh,pkh->pjk/dot_general | solution.py:80
  588.4 0.6 iota_add_fusion.6
  589.1 16.2 %fusion.108 = f32[512,8,32]{0,2,1:T(8,128)S(1)} fusion(bf16[8,32,2048]{2,1,0:T(8,128)(2,1)S(1)} %get-tuple-element.235, s32[2048]{0:T(1024)S(1)} %add.229, s32[512]{0:T(512)S(1)} %iota_add_fusion.6, f32[2048]{0:T(1024)S(1)} %compare_select_fusion.4), kind=kOutput, calls=%fused_computation.16.clone.1 | convolution fusion | flops 553648128 | bytes 1591296 | tf_op jit(solution)/shard_map/while/body/eval_jaxpr/jh,pkh->pjk/dot_general | solution.py:85
  605.2 16.9 %fusion.109 = f32[8,8,512,32]{2,3,1,0:T(8,128)} fusion(f32[8,8,512,32]{2,3,1,0:T(8,128)} %get-tuple-element.225, s32[]{:T(128)} %get-tuple-element.223, f32[512,8,32]{0,2,1:T(8,128)S(1)} %fusion.108, bf16[8,32,2048]{2,1,0:T(8,128)(2,1)S(1)} %get-tuple-element.236, s32[2048]{0:T(1024)S(1)} %add.229, s32[512]{0:T(512)S(1)} %iota_add_fusion.6, ...), kind=kOutput, calls=%fused_computation.29.clone.1 | convolution fusion | flops 553779200 | bytes 2116096 | tf_op jit(solution)/shard_map/while/body/eval_jaxpr/jh,pkh->pjk/dot_general | solution.py:83
  622.1 16.0 %fusion.106 = f32[512,8,32]{0,2,1:T(8,128)S(1)} fusion(bf16[8,32,2048]{2,1,0:T(8,128)(2,1)S(1)} %get-tuple-element.236, s32[2048]{0:T(1024)S(1)} %add.229, s32[512]{0:T(512)S(1)} %iota_add_fusion.6, f32[2048]{0:T(1024)S(1)} %compare_select_fusion.4), kind=kOutput, calls=%fused_computation.17.clone.1 | convolution fusion | flops 553648128 | bytes 1591296 | tf_op jit(solution)/shard_map/while/body/eval_jaxpr/jh,pkh->pjk/dot_general | solution.py:82
  638.1 18.8 %fusion.107 = f32[8,8,512,32]{2,3,1,0:T(8,128)} fusion(f32[8,8,512,32]{2,3,1,0:T(8,128)} %get-tuple-element.224, s32[]{:T(128)} %get-tuple-element.223, f32[512,8,32]{0,2,1:T(8,128)S(1)} %fusion.106, bf16[8,32,2048]{2,1,0:T(8,128)(2,1)S(1)} %get-tuple-element.235, s32[2048]{0:T(1024)S(1)} %add.229, s32[512]{0:T(512)S(1)} %iota_add_fusion.6, ...), kind=kOutput, calls=%fused_computation.26.clone.1 | convolution fusion | flops 553779200 | bytes 2116096 | tf_op jit(solution)/shard_map/while/body/eval_jaxpr/jh,pkh->pjk/dot_general | solution.py:80
  657.8 0.6 iota_add_fusion.6
  658.5 16.2 %fusion.108 = f32[512,8,32]{0,2,1:T(8,128)S(1)} fusion(bf16[8,32,2048]{2,1,0:T(8,128)(2,1)S(1)} %get-tuple-element.235, s32[2048]{0:T(1024)S(1)} %add.229, s32[512]{0:T(512)S(1)} %iota_add_fusion.6, f32[2048]{0:T(1024)S(1)} %compare_select_fusion.4), kind=kOutput, calls=%fused_computation.16.clone.1 | convolution fusion | flops 553648128 | bytes 1591296 | tf_op jit(solution)/shard_map/while/body/eval_jaxpr/jh,pkh->pjk/dot_general | solution.py:85
  674.7 16.9 %fusion.109 = f32[8,8,512,32]{2,3,1,0:T(8,128)} fusion(f32[8,8,512,32]{2,3,1,0:T(8,128)} %get-tuple-element.225, s32[]{:T(128)} %get-tuple-element.223, f32[512,8,32]{0,2,1:T(8,128)S(1)} %fusion.108, bf16[8,32,2048]{2,1,0:T(8,128)(2,1)S(1)} %get-tuple-element.236, s32[2048]{0:T(1024)S(1)} %add.229, s32[512]{0:T(512)S(1)} %iota_add_fusion.6, ...), kind=kOutput, calls=%fused_computation.29.clone.1 | convolution fusion | flops 553779200 | bytes 2116096 | tf_op jit(solution)/shard_map/while/body/eval_jaxpr/jh,pkh->pjk/dot_general | solution.py:83
  691.5 16.0 %fusion.106 = f32[512,8,32]{0,2,1:T(8,128)S(1)} fusion(bf16[8,32,2048]{2,1,0:T(8,128)(2,1)S(1)} %get-tuple-element.236, s32[2048]{0:T(1024)S(1)} %add.229, s32[512]{0:T(512)S(1)} %iota_add_fusion.6, f32[2048]{0:T(1024)S(1)} %compare_select_fusion.4), kind=kOutput, calls=%fused_computation.17.clone.1 | convolution fusion | flops 553648128 | bytes 1591296 | tf_op jit(solution)/shard_map/while/body/eval_jaxpr/jh,pkh->pjk/dot_general | solution.py:82
  707.5 18.8 %fusion.107 = f32[8,8,512,32]{2,3,1,0:T(8,128)} fusion(f32[8,8,512,32]{2,3,1,0:T(8,128)} %get-tuple-element.224, s32[]{:T(128)} %get-tuple-element.223, f32[512,8,32]{0,2,1:T(8,128)S(1)} %fusion.106, bf16[8,32,2048]{2,1,0:T(8,128)(2,1)S(1)} %get-tuple-element.235, s32[2048]{0:T(1024)S(1)} %add.229, s32[512]{0:T(512)S(1)} %iota_add_fusion.6, ...), kind=kOutput, calls=%fused_computation.26.clone.1 | convolution fusion | flops 553779200 | bytes 2116096 | tf_op jit(solution)/shard_map/while/body/eval_jaxpr/jh,pkh->pjk/dot_general | solution.py:80
  727.3 0.6 iota_add_fusion.6
  727.9 16.2 %fusion.108 = f32[512,8,32]{0,2,1:T(8,128)S(1)} fusion(bf16[8,32,2048]{2,1,0:T(8,128)(2,1)S(1)} %get-tuple-element.235, s32[2048]{0:T(1024)S(1)} %add.229, s32[512]{0:T(512)S(1)} %iota_add_fusion.6, f32[2048]{0:T(1024)S(1)} %compare_select_fusion.4), kind=kOutput, calls=%fused_computation.16.clone.1 | convolution fusion | flops 553648128 | bytes 1591296 | tf_op jit(solution)/shard_map/while/body/eval_jaxpr/jh,pkh->pjk/dot_general | solution.py:85
  744.1 16.9 %fusion.109 = f32[8,8,512,32]{2,3,1,0:T(8,128)} fusion(f32[8,8,512,32]{2,3,1,0:T(8,128)} %get-tuple-element.225, s32[]{:T(128)} %get-tuple-element.223, f32[512,8,32]{0,2,1:T(8,128)S(1)} %fusion.108, bf16[8,32,2048]{2,1,0:T(8,128)(2,1)S(1)} %get-tuple-element.236, s32[2048]{0:T(1024)S(1)} %add.229, s32[512]{0:T(512)S(1)} %iota_add_fusion.6, ...), kind=kOutput, calls=%fused_computation.29.clone.1 | convolution fusion | flops 553779200 | bytes 2116096 | tf_op jit(solution)/shard_map/while/body/eval_jaxpr/jh,pkh->pjk/dot_general | solution.py:83
  761.0 16.0 %fusion.106 = f32[512,8,32]{0,2,1:T(8,128)S(1)} fusion(bf16[8,32,2048]{2,1,0:T(8,128)(2,1)S(1)} %get-tuple-element.236, s32[2048]{0:T(1024)S(1)} %add.229, s32[512]{0:T(512)S(1)} %iota_add_fusion.6, f32[2048]{0:T(1024)S(1)} %compare_select_fusion.4), kind=kOutput, calls=%fused_computation.17.clone.1 | convolution fusion | flops 553648128 | bytes 1591296 | tf_op jit(solution)/shard_map/while/body/eval_jaxpr/jh,pkh->pjk/dot_general | solution.py:82
  776.9 18.8 %fusion.107 = f32[8,8,512,32]{2,3,1,0:T(8,128)} fusion(f32[8,8,512,32]{2,3,1,0:T(8,128)} %get-tuple-element.224, s32[]{:T(128)} %get-tuple-element.223, f32[512,8,32]{0,2,1:T(8,128)S(1)} %fusion.106, bf16[8,32,2048]{2,1,0:T(8,128)(2,1)S(1)} %get-tuple-element.235, s32[2048]{0:T(1024)S(1)} %add.229, s32[512]{0:T(512)S(1)} %iota_add_fusion.6, ...), kind=kOutput, calls=%fused_computation.26.clone.1 | convolution fusion | flops 553779200 | bytes 2116096 | tf_op jit(solution)/shard_map/while/body/eval_jaxpr/jh,pkh->pjk/dot_general | solution.py:80
  796.7 0.6 iota_add_fusion.6
  797.3 16.2 %fusion.108 = f32[512,8,32]{0,2,1:T(8,128)S(1)} fusion(bf16[8,32,2048]{2,1,0:T(8,128)(2,1)S(1)} %get-tuple-element.235, s32[2048]{0:T(1024)S(1)} %add.229, s32[512]{0:T(512)S(1)} %iota_add_fusion.6, f32[2048]{0:T(1024)S(1)} %compare_select_fusion.4), kind=kOutput, calls=%fused_computation.16.clone.1 | convolution fusion | flops 553648128 | bytes 1591296 | tf_op jit(solution)/shard_map/while/body/eval_jaxpr/jh,pkh->pjk/dot_general | solution.py:85
  813.5 16.9 %fusion.109 = f32[8,8,512,32]{2,3,1,0:T(8,128)} fusion(f32[8,8,512,32]{2,3,1,0:T(8,128)} %get-tuple-element.225, s32[]{:T(128)} %get-tuple-element.223, f32[512,8,32]{0,2,1:T(8,128)S(1)} %fusion.108, bf16[8,32,2048]{2,1,0:T(8,128)(2,1)S(1)} %get-tuple-element.236, s32[2048]{0:T(1024)S(1)} %add.229, s32[512]{0:T(512)S(1)} %iota_add_fusion.6, ...), kind=kOutput, calls=%fused_computation.29.clone.1 | convolution fusion | flops 553779200 | bytes 2116096 | tf_op jit(solution)/shard_map/while/body/eval_jaxpr/jh,pkh->pjk/dot_general | solution.py:83
  830.3 16.0 %fusion.106 = f32[512,8,32]{0,2,1:T(8,128)S(1)} fusion(bf16[8,32,2048]{2,1,0:T(8,128)(2,1)S(1)} %get-tuple-element.236, s32[2048]{0:T(1024)S(1)} %add.229, s32[512]{0:T(512)S(1)} %iota_add_fusion.6, f32[2048]{0:T(1024)S(1)} %compare_select_fusion.4), kind=kOutput, calls=%fused_computation.17.clone.1 | convolution fusion | flops 553648128 | bytes 1591296 | tf_op jit(solution)/shard_map/while/body/eval_jaxpr/jh,pkh->pjk/dot_general | solution.py:82
  846.3 18.8 %fusion.107 = f32[8,8,512,32]{2,3,1,0:T(8,128)} fusion(f32[8,8,512,32]{2,3,1,0:T(8,128)} %get-tuple-element.224, s32[]{:T(128)} %get-tuple-element.223, f32[512,8,32]{0,2,1:T(8,128)S(1)} %fusion.106, bf16[8,32,2048]{2,1,0:T(8,128)(2,1)S(1)} %get-tuple-element.235, s32[2048]{0:T(1024)S(1)} %add.229, s32[512]{0:T(512)S(1)} %iota_add_fusion.6, ...), kind=kOutput, calls=%fused_computation.26.clone.1 | convolution fusion | flops 553779200 | bytes 2116096 | tf_op jit(solution)/shard_map/while/body/eval_jaxpr/jh,pkh->pjk/dot_general | solution.py:80
  868.0 10.5 copy.27
  878.5 10.5 copy.28
  889.0 118.7 %gather_fusion = f32[8192,32]{1,0:T(8,128)} fusion(f32[8,4096,32]{2,1,0:T(8,128)} %bitcast.135, s32[8192]{0:T(1024)S(1)} %bitcast.133), kind=kCustom, calls=%fused_computation | custom fusion | bytes 2162688 | tf_op jit(solution)/shard_map/vmap()/gather | solution.py:93
  1007.7 118.7 %gather_fusion.1 = f32[8192,32]{1,0:T(8,128)} fusion(f32[8,4096,32]{2,1,0:T(8,128)} %bitcast.136, s32[8192]{0:T(1024)S(1)} %bitcast.134), kind=kCustom, calls=%fused_computation.1 | custom fusion | bytes 2162688 | tf_op jit(solution)/shard_map/vmap()/gather | solution.py:93
  1126.4 21.6 %multiply_reduce_fusion = f32[8,1024]{1,0:T(8,128)} fusion(f32[8,1024,32]{2,1,0:T(8,128)} %bitcast.142, f32[8,1024,32]{2,1,0:T(8,128)} %bitcast.141, s32[8,1024]{1,0:T(8,128)S(1)} %copy-done.2, f32[32]{0:T(128)S(1)} %copy-done.4), kind=kLoop, calls=%fused_computation.75 | loop fusion | flops 4972544 | bytes 2162816 | tf_op jit(solution)/shard_map/reduce_sum | solution.py:25
  (63 shorter events, 7.2 us)
Async XLA Ops:
  6.5 3.8 copy-start.5
  6.5 136.1 %all-gather.2.cloned.1.call-start = ((), (), s32[]{:S(2)}) async-start(), calls=%async_computation.1 | async-start | bytes 17825792 | tf_op jit(solution)/shard_map/all_gather | solution.py:52
  11.9 8.5 copy-start.1
  166.3 36.8 %slice-start = ((s8[8388608]{0:T(1024)(128)(4,1)}), s8[4194304]{0:T(1024)(128)(4,1)S(1)}, s32[]{:S(2)}) async-start(s8[8388608]{0:T(1024)(128)(4,1)} %bitcast.139), calls=%async_computation.2 | async-start | bytes 8388608
  182.9 20.2 %slice-start.1 = ((s8[8388608]{0:T(1024)(128)(4,1)}), s8[4194304]{0:T(1024)(128)(4,1)S(1)}, s32[]{:S(2)}) async-start(s8[8388608]{0:T(1024)(128)(4,1)} %bitcast.139), calls=%async_computation.3 | async-start | bytes 8388608
  182.9 20.2 %copy-start = (bf16[2048,1,64,32]{0,2,1,3:T(8,128)(2,1)S(1)}, bf16[2048,1,64,32]{0,2,1,3:T(8,128)(2,1)}, u32[]{:S(2)}) copy-start(bf16[2048,1,64,32]{0,2,1,3:T(8,128)(2,1)} %copy_negate_fusion) | copy-start | bytes 25165828
  256.4 11.6 %copy-start.3 = (s32[8,1024]{1,0:T(8,128)S(1)}, s32[8,1024]{1,0:T(8,128)}, u32[]{:S(2)}) copy-start(s32[8,1024]{1,0:T(8,128)} %param.11) | copy-start | bytes 98308
  264.2 44.8 %all-to-all-start = ((bf16[128,2,32,128]{3,2,1,0:T(8,128)(2,1)}), bf16[128,2,32,128]{3,2,1,0:T(8,128)(2,1)S(1)}, u32[]{:S(2)}, u32[]{:S(2)}) async-start(bf16[128,2,32,128]{3,2,1,0:T(8,128)(2,1)} %convert_element_type.48), calls=%async_computation | async-start | bytes 4194304 | tf_op jit(solution)/shard_map/all_to_all | solution.py:64
  1007.7 118.7 %copy-start.2 = (s32[8,1024]{1,0:T(8,128)S(1)}, s32[8,1024]{1,0:T(8,128)}, u32[]{:S(2)}) copy-start(s32[8,1024]{1,0:T(8,128)} %add_select_fusion.2) | copy-start | bytes 98308
  1007.7 118.7 %copy-start.4 = (f32[32]{0:T(128)S(1)}, f32[32]{0:T(128)}, u32[]{:S(2)}) copy-start(f32[32]{0:T(128)} %compare_select_fusion.2) | copy-start | bytes 388
Sparse Core Ops, SparseCore 0:
  9.5 133.0 all-gather.1
where the time goes:
time: 1170 us; the launch traced here: 1160 us
  matrix products  582 us (50%)
  local copies, waits for them, and re-layouts  326 us (28%)
  waiting for transfers between devices  124 us (11%)
  other arithmetic  100 us (9%)
  between operations  13.8 us (1%)
    gather x2, local copies, waits for them, and re-layouts, pick_rows(): return grid_table[pixel_rows]  237 us
    dot_general x8, matrix products, grid_rows(): jnp.einsum('jh,pkh->pjk', cos_part, spin_re, preferred_element_type=jnp.f...  150 us
    dot_general x8, matrix products, grid_rows(): jnp.einsum('jh,pkh->pjk', cos_part, spin_im, preferred_element_type=jnp.f...  135 us
    dot_general x8, matrix products, grid_rows(): jnp.einsum('jh,pkh->pjk', sin_part, spin_re, preferred_element_type=jnp.f...  129 us
    dot_general x8, matrix products, grid_rows(): jnp.einsum('jh,pkh->pjk', sin_part, spin_im, preferred_element_type=jnp.f...  128 us
    all_gather x1, waiting for transfers between devices, body(): beam_piece = lax.all_gather(beam, 'sky', axis=0, tiled=True)  84.3 us
    dot_general x1, matrix products, body(): jnp.einsum('xbrkil,xlcdk->rdckbi', coeff_both, beam_block, preferred_elem...  40.2 us
    all_to_all x1, waiting for transfers between devices, body(): lax.all_to_all(spin_sums, 'sky', split_axis=0, concat_axis=3, tiled=True)  39.8 us
  transfers between devices with their start and end apart: 2, of which 2 were waited for; matrix products, arithmetic and copies ran while one was open for 4% of the time, Pallas kernels for 0%

commit v1 on v0

v1 whole, which is shorter than its diff:
```python
import functools
import math

import jax
import jax.numpy as jnp
from jax import lax
from jax.experimental import pallas as pl
from jax.experimental.pallas import tpu as pltpu
from jax.sharding import PartitionSpec as P

CHUNKS = 4
ROWS = 8
VMEM_LIMIT = 48 * 1024 * 1024


def sincos(index, period):
    quarter = period // 4
    index = index & (period - 1)
    shifted = index + quarter // 2
    quadrant = (shifted >> (quarter.bit_length() - 1)) & 3
    rest = (shifted & (quarter - 1)) - quarter // 2
    x = rest.astype(jnp.float32) * (2.0 * math.pi / period)
    y = x * x
    s = x * (1.0 + y * (-1.0 / 6 + y * (1.0 / 120 + y * (-1.0 / 5040 + y * (1.0 / 362880)))))
    c = 1.0 + y * (-0.5 + y * (1.0 / 24 + y * (-1.0 / 720 + y * (1.0 / 40320))))
    odd = (quadrant & 1) == 1
    cos_size = jnp.where(odd, s, c)
    sin_size = jnp.where(odd, c, s)
    cos_value = jnp.where((quadrant == 1) | (quadrant == 2), -cos_size, cos_size)
    sin_value = jnp.where(quadrant >= 2, -sin_size, sin_size)
    return cos_value, sin_value


def phase_kernel(cycle_pixels, orient_bins, pointing_ref, phase_ref, orient_ref):
    samples = pointing_ref.shape[1]
    block_size = phase_ref.shape[1] // 2
    step = cycle_pixels // orient_bins
    low = lax.broadcasted_iota(jnp.int32, (ROWS, samples), 0)
    for j in range(pointing_ref.shape[0]):
        point = pointing_ref[pl.ds(j, 1), :]
        pixel = jnp.broadcast_to(point // orient_bins, (ROWS, samples))
        orient = jnp.broadcast_to(point & (orient_bins - 1), (ROWS, samples))
        base_cos, base_sin = sincos(low * pixel, cycle_pixels)
        if block_size == ROWS:
            cos_rows = [base_cos]
            sin_rows = [base_sin]
        else:
            cos_rows = []
            sin_rows = []
            outer_cos, outer_sin = sincos(low * ROWS * pixel, cycle_pixels)
            for a in range(block_size // ROWS):
                oc = outer_cos[a : a + 1]
                os = outer_sin[a : a + 1]
                cos_rows.append(oc * base_cos - os * base_sin)
                sin_rows.append(os * base_cos + oc * base_sin)
        phase_ref[j] = jnp.concatenate(cos_rows + sin_rows, axis=0).astype(jnp.bfloat16)
        orient_cos, orient_sin = sincos(low * orient * step, cycle_pixels)
        orient_ref[j] = jnp.concatenate([orient_cos, orient_sin], axis=0)


def spin_kernel(first_k, order_ref, wigner_ref, sky_ref, beam_ref, out_ref, coeff):
    blocks, cycles, _, block_size, degrees = wigner_ref.shape
    lanes = beam_ref.shape[-1]
    half = blocks * cycles * block_size
    for b in range(blocks):
        for r in range(cycles):
            table = wigner_ref[b, r, 0]
            row = (b * cycles + r) * block_size
            for c in range(2):
                coeff[c * half + row : c * half + row + block_size, :] = table * sky_ref[b, c]
    beam = beam_ref[...].reshape(degrees, lanes)
    sums = jnp.dot(coeff[...], beam, preferred_element_type=jnp.float32)
    sign = jnp.where(
        lax.broadcasted_iota(jnp.int32, (half, lanes), 1) < lanes // 2, -1.0, 1.0
    ).astype(jnp.float32)
    spin = sums[:half] + sign * pltpu.roll(sums[half:], lanes // 2, 1)
    spin = spin.astype(jnp.bfloat16).astype(jnp.float32)
    k_weight = jnp.where(first_k + pl.program_id(0) == 0, 1.0, 2.0).astype(jnp.float32)
    turned = sign * pltpu.roll(spin, lanes // 2, 1)
    slot = lax.broadcasted_iota(jnp.int32, (block_size, lanes), 0)
    for b in range(blocks):
        weight = jnp.where(order_ref[b] * block_size + slot == 0, 1.0, 2.0) * k_weight
        for r in range(cycles):
            row = (b * cycles + r) * block_size
            both = jnp.concatenate(
                [spin[row : row + block_size] * weight, turned[row : row + block_size] * weight],
                axis=0,
            )
            out_ref[r, b, 0] = both.T


def stream_kernel(first_k, spins, cycle_pixels, orient_bins, detectors, block_size, order_ref,
                  spin_ref, phase_ref, orient_ref, pointing_ref, before_ref, out_ref):
    samples = pointing_ref.shape[1]
    blocks = order_ref.shape[0]
    step = cycle_pixels // orient_bins
    groups = spins // ROWS
    first = pl.program_id(1) * pointing_ref.shape[0]
    row_id = lax.broadcasted_iota(jnp.int32, (max(ROWS, blocks * groups), samples), 0)
    k_outer = (first_k + (row_id % groups) * ROWS) * step
    m_outer = jnp.zeros_like(row_id)
    for b in range(blocks):
        m_outer = jnp.where(row_id // groups == b, order_ref[b] * block_size, m_outer)
    for j in range(pointing_ref.shape[0]):
        point = pointing_ref[pl.ds(j, 1), :]
        pixel = point // orient_bins
        orient = point & (orient_bins - 1)
        outer_cos, outer_sin = sincos(k_outer * orient + m_outer * pixel, cycle_pixels)
        base_cos = orient_ref[j, :ROWS]
        base_sin = orient_ref[j, ROWS:]
        count = blocks * spins
        real_rows = spin_ref[0, pl.ds(first + j, count, stride=2 * detectors), :]
        imag_rows = spin_ref[0, pl.ds(first + j + detectors, count, stride=2 * detectors), :]
        rows = jnp.concatenate([real_rows, imag_rows], axis=0).astype(jnp.bfloat16)
        cycle = jnp.dot(rows, phase_ref[j], preferred_element_type=jnp.float32)
        total = jnp.zeros((ROWS, samples), jnp.float32)
        for g in range(blocks * groups):
            oc = outer_cos[g : g + 1]
            os = outer_sin[g : g + 1]
            real = cycle[g * ROWS : (g + 1) * ROWS]
            imag = cycle[count + g * ROWS : count + (g + 1) * ROWS]
            total += real * (oc * base_cos - os * base_sin)
            total -= imag * (os * base_cos + oc * base_sin)
        out_ref[pl.ds(j, 1), :] = before_ref[pl.ds(j, 1), :] + jnp.sum(total, axis=0, keepdims=True)


def body(wigner, sky_blocks, beam, block_order, pointing):
    device = lax.axis_index("sky")
    blocks, cycles, spins, block_size, degrees = wigner.shape
    degrees_here = beam.shape[0]
    lanes = beam.shape[1] // spins
    detectors = lanes // 2
    cycle_pixels = 2 * degrees
    orient_bins = 4 * spins
    pairs = cycles * detectors
    samples = pointing.shape[1]
    chunk = spins // CHUNKS
    params = pltpu.CompilerParams(vmem_limit_bytes=VMEM_LIMIT)

    degree = jnp.arange(degrees, dtype=jnp.int32)
    own_blocks = lax.dynamic_slice_in_dim(block_order, device * blocks, blocks)
    order = own_blocks[:, None] * block_size + jnp.arange(block_size, dtype=jnp.int32)
    sky = jnp.where(degree >= order[:, None, :, None], sky_blocks, jnp.bfloat16(0))

    points = lax.all_gather(pointing, "sky", axis=0, tiled=True)
    turned = jnp.transpose(beam.reshape(degrees_here, lanes, spins), (2, 0, 1))
    here = device * degrees_here + jnp.arange(degrees_here, dtype=jnp.int32)
    k_index = jnp.arange(spins, dtype=jnp.int32)
    turned = jnp.where(here[None, :, None] >= k_index[:, None, None], turned, jnp.bfloat16(0))

    gathered = [
        lax.all_gather(turned[c * chunk : (c + 1) * chunk], "sky", axis=0, tiled=False)
        for c in range(CHUNKS)
    ]

    phases, orients = pl.pallas_call(
        functools.partial(phase_kernel, cycle_pixels, orient_bins),
        grid=(pairs // ROWS,),
        in_specs=[pl.BlockSpec((ROWS, samples), lambda p: (p, 0))],
        out_specs=[
            pl.BlockSpec((ROWS, 2 * block_size, samples), lambda p: (p, 0, 0)),
            pl.BlockSpec((ROWS, 2 * ROWS, samples), lambda p: (p, 0, 0)),
        ],
        out_shape=[
            jax.ShapeDtypeStruct((pairs, 2 * block_size, samples), jnp.bfloat16),
            jax.ShapeDtypeStruct((pairs, 2 * ROWS, samples), jnp.float32),
        ],
        compiler_params=params,
        cost_estimate=pl.CostEstimate(flops=10**10, bytes_accessed=5 * 10**7, transcendentals=0),
        name="phases",
    )(points)

    count = blocks * chunk * lanes
    stream = jnp.zeros((pairs, samples), jnp.float32)
    for c in range(CHUNKS):
        first_k = c * chunk
        spin_sums = pl.pallas_call(
            functools.partial(spin_kernel, first_k),
            grid=(chunk,),
            in_specs=[
                pl.BlockSpec(memory_space=pltpu.SMEM),
                pl.BlockSpec(
                    (blocks, cycles, 1, block_size, degrees),
                    lambda k, first_k=first_k: (0, 0, first_k + k, 0, 0),
                ),
                pl.BlockSpec((blocks, 2, block_size, degrees), lambda k: (0, 0, 0, 0)),
                pl.BlockSpec(
                    (degrees // degrees_here, 1, degrees_here, lanes), lambda k: (0, k, 0, 0)
                ),
            ],
            out_specs=pl.BlockSpec(
                (cycles, blocks, 1, lanes, 2 * block_size), lambda k: (0, 0, k, 0, 0)
            ),
            out_shape=jax.ShapeDtypeStruct(
                (cycles, blocks, chunk, lanes, 2 * block_size), jnp.float32
            ),
            scratch_shapes=[
                pltpu.VMEM((2 * blocks * cycles * block_size, degrees), jnp.bfloat16)
            ],
            compiler_params=params,
            cost_estimate=pl.CostEstimate(
                flops=4 * 10**9, bytes_accessed=2 * 10**7, transcendentals=0
            ),
            name=f"spin_{c}",
        )(own_blocks, wigner, sky, gathered[c])
        spin_sums = spin_sums.reshape(cycles, count, 2 * block_size)
        row_of = lambda r, e: (r * (detectors // ROWS) + e, 0)
        pair_of = lambda r, e: (r * (detectors // ROWS) + e, 0, 0)
        stream = pl.pallas_call(
            functools.partial(
                stream_kernel, first_k, chunk, cycle_pixels, orient_bins, detectors, block_size
            ),
            grid=(cycles, detectors // ROWS),
            in_specs=[
                pl.BlockSpec(memory_space=pltpu.SMEM),
                pl.BlockSpec((1, count, 2 * block_size), lambda r, e: (r, 0, 0)),
                pl.BlockSpec((ROWS, 2 * block_size, samples), pair_of),
                pl.BlockSpec((ROWS, 2 * ROWS, samples), pair_of),
                pl.BlockSpec((ROWS, samples), row_of),
                pl.BlockSpec((ROWS, samples), row_of),
            ],
            out_specs=pl.BlockSpec((ROWS, samples), row_of),
            out_shape=jax.ShapeDtypeStruct((pairs, samples), jnp.float32),
            compiler_params=params,
            cost_estimate=pl.CostEstimate(
                flops=6 * 10**9, bytes_accessed=4 * 10**7, transcendentals=0
            ),
            name=f"stream_{c}",
        )(own_blocks, spin_sums, phases, orients, points, stream)

    return lax.psum_scatter(stream, "sky", scatter_dimension=0, tiled=True)


def solution(mesh):
    return jax.shard_map(
        body,
        mesh=mesh,
        in_specs=(
            P("sky", None, None, None, None),
            P("sky", None, None, None),
            P("sky", "groups"),
            P(),
            P(("groups", "sky"), None),
        ),
        out_specs=P(("groups", "sky"), None),
        check_vma=False,
    )
```

time: 1170 us -> 402 us (0.34); the launches traced: 1160 us -> 399 us
  matrix products: 582 us -> 0 us
  local copies, waits for them, and re-layouts: 326 us -> 34.4 us
  Pallas kernels: 0 us -> 167 us
  other arithmetic: 100 us -> 0.57 us
  waiting for transfers between devices: 124 us -> 158 us
  blocking collectives: 0 us -> 25.6 us
    dot_general x33 -> x0, matrix products: 582 us -> none  [the longest x8 150 us: grid_rows(): jnp.einsum('jh,pkh->pjk', cos_part, spin_re, preferred_element_type=jnp.f...]
    gather x2 -> x0, local copies, waits for them, and re-layouts: 237 us -> none  [pick_rows(): return grid_table[pixel_rows]]
    pallas_call x0 -> x9, Pallas kernels: none -> 167 us  [the longest x4 93.5 us: body(): pl.pallas_call(functools.partial(stream_kernel, first_k, chunk, cycle_pix...]
    reduce_scatter x0 -> x1, waiting for transfers between devices: none -> 54 us  [body(): return lax.psum_scatter(stream, 'sky', scatter_dimension=0, tiled=True)]
    another operation x4 -> x0, other arithmetic: 44.6 us -> none  [the longest x1 37.8 us: body(): coeff_both = jnp.stack([coeff_re, coeff_im], axis=0)]
    all_to_all x1 -> x0, waiting for transfers between devices: 39.8 us -> none  [body(): lax.all_to_all(spin_sums, 'sky', split_axis=0, concat_axis=3, tiled=True)]
    all_gather x0 -> x4, local copies, waits for them, and re-layouts: none -> 27.6 us  [body(): lax.all_gather(turned[c * chunk:(c + 1) * chunk], 'sky', axis=0, tiled=Fa...]
    all_gather x0 -> x1, blocking collectives: none -> 25.6 us  [body(): points = lax.all_gather(pointing, 'sky', axis=0, tiled=True)]
  transfers between devices with their start and end apart: 2 -> 5, of which waited for: 2 -> 4; matrix products, arithmetic and copies ran while one was open for 4% -> 5% of each run, Pallas kernels for 0% -> 16%
where the time goes in v1:
time: 402 us; the launch traced here: 399 us
  Pallas kernels  167 us (42%)
  waiting for transfers between devices  158 us (39%)
  local copies, waits for them, and re-layouts  34.4 us (9%)
  blocking collectives  25.6 us (6%)
  between operations  13.3 us (3%)
    all_gather x4, waiting for transfers between devices, body(): lax.all_gather(turned[c * chunk:(c + 1) * chunk], 'sky', axis=0, tiled=Fa...  102 us
    pallas_call x4, Pallas kernels, body(): pl.pallas_call(functools.partial(stream_kernel, first_k, chunk, cycle_pix...  93.5 us
    reduce_scatter x1, waiting for transfers between devices, body(): return lax.psum_scatter(stream, 'sky', scatter_dimension=0, tiled=True)  54 us
    pallas_call x4, Pallas kernels, body(): pl.pallas_call(functools.partial(spin_kernel, first_k), grid=(chunk,), in...  43.1 us
    pallas_call x1, Pallas kernels, body(): pl.pallas_call(functools.partial(phase_kernel, cycle_pixels, orient_bins)...  30.6 us
    all_gather x4, local copies, waits for them, and re-layouts, body(): lax.all_gather(turned[c * chunk:(c + 1) * chunk], 'sky', axis=0, tiled=Fa...  27.6 us
    all_gather x1, blocking collectives, body(): points = lax.all_gather(pointing, 'sky', axis=0, tiled=True)  25.6 us
  transfers between devices with their start and end apart: 5, of which 4 were waited for; matrix products, arithmetic and copies ran while one was open for 5% of the time, Pallas kernels for 16%

profile of v1, /device:TPU:0, one launch (start us, length us, event | category | flops | bytes accessed | tf_op | source)
XLA Modules:
  0.0 399.2 jit_solution(10282791918574568719)
XLA Ops:
  6.5 0.0 copy-start.8
  6.5 0.0 copy-start.7
  6.5 0.0 copy-start.6
  6.5 0.0 all-gather.15.cloned.1.call-start
  6.6 1.7 copy.7
  8.3 0.1 broadcast_select_fusion
  8.4 1.1 fusion
  9.4 0.0 all-gather.15.cloned.1.call-update
  9.4 0.0 all-gather.13.cloned.1.call-start
  9.5 0.7 all-gather.13.cloned.1.call-update
  10.2 0.0 all-gather.11.cloned.1.call-start
  10.2 0.7 all-gather.11.cloned.1.call-update
  10.9 0.0 all-gather.9.cloned.1.call-start
  11.0 0.5 all-gather.9.cloned.1.call-update
  11.5 0.0 reduce-scatter.2.cloned.1.call-start
  11.6 0.0 copy-done.8
  11.6 0.1 broadcast_multiply_fusion
  11.6 0.1 iota_add_fusion
  11.7 0.0 copy-done.7
  11.7 25.6 %all_gather.29.pointing_ref = s32[128,1024]{1,0:T(8,128)S(1)} all-gather(s32[8,1024]{1,0:T(8,128)S(1)} %copy-done.7), channel_id=1, replica_groups=mesh['groups'=2,'sky'=16] {'sky'}, dimensions={0}, use_global_device_ids=true | all-gather | bytes 557056 | tf_op jit(solution)/shard_map/all_gather | solution.py:145
  37.3 0.2 iota_compare_fusion
  37.5 0.0 copy-done.6
  37.5 0.1 broadcast_select_fusion.1.sky_ref
  37.6 30.6 %phases.1 = (bf16[128,128,1024]{2,1,0:T(8,128)(2,1)}, f32[128,16,1024]{2,1,0:T(8,128)}) custom-call(s32[128,1024]{1,0:T(8,128)S(1)} %all_gather.29.pointing_ref), custom_call_target="tpu_custom_call" | custom-call | flops 10000000000 | bytes 50000000 | tf_op jit(solution)/shard_map/phases/pallas_call | solution.py:156
  68.2 0.0 all-gather.15.cloned.1.call-done
  68.2 6.9 %copy.11 = bf16[128,128,128]{2,1,0:T(8,128)(2,1)} copy(bf16[128,128,128]{1,0,2:T(8,128)(2,1)} %all-gather.15.cloned.1.call-done) | data formatting | bytes 8388608 | tf_op jit(solution)/shard_map/all_gather | solution.py:152
  75.1 45.1 %all-gather.13.cloned.1.call-done = bf16[128,128,128]{1,0,2:T(8,128)(2,1)} async-done(((bf16[8,128,128]{1,0,2:T(8,128)(2,1)}), bf16[128,128,128]{1,0,2:T(8,128)(2,1)}) %all-gather.13.cloned.1.call-update) | async-done | bytes 4194320 | tf_op jit(solution)/shard_map/all_gather | solution.py:152
  120.2 6.9 %copy.10 = bf16[128,128,128]{2,1,0:T(8,128)(2,1)} copy(bf16[128,128,128]{1,0,2:T(8,128)(2,1)} %all-gather.13.cloned.1.call-done) | data formatting | bytes 8388608 | tf_op jit(solution)/shard_map/all_gather | solution.py:152
  127.1 46.7 %all-gather.11.cloned.1.call-done = bf16[128,128,128]{1,0,2:T(8,128)(2,1)} async-done(((bf16[8,128,128]{1,0,2:T(8,128)(2,1)}), bf16[128,128,128]{1,0,2:T(8,128)(2,1)}) %all-gather.11.cloned.1.call-update) | async-done | bytes 4194320 | tf_op jit(solution)/shard_map/all_gather | solution.py:152
  173.8 6.9 %copy.9 = bf16[128,128,128]{2,1,0:T(8,128)(2,1)} copy(bf16[128,128,128]{1,0,2:T(8,128)(2,1)} %all-gather.11.cloned.1.call-done) | data formatting | bytes 8388608 | tf_op jit(solution)/shard_map/all_gather | solution.py:152
  180.7 10.7 %spin_0.1 = f32[2,2,8,128,128]{4,3,2,1,0:T(8,128)S(1)} custom-call(s32[2]{0:T(128)S(1)} %get-tuple-element.10.order_ref, bf16[2,2,32,64,2048]{4,3,2,1,0:T(8,128)(2,1)} %wigner_ref.7, bf16[2,2,64,2048]{3,2,1,0:T(8,128)(2,1)S(1)} %broadcast_select_fusion.1.sky_ref, bf16[16,8,128,128]{3,2,1,0:T(8,128)(2,1)} %bitcast.15), custom_call_target="tpu_custom_call" | custom-call | flops 4000000000 | bytes 20000000 | tf_op jit(solution)/shard_map/spin_0/pallas_call | solution.py:177
  191.4 0.0 copy-start.4
  191.4 1.4 copy-done.4
  192.8 10.8 %spin_1.1 = f32[2,2,8,128,128]{4,3,2,1,0:T(8,128)S(1)} custom-call(s32[2]{0:T(128)S(1)} %get-tuple-element.10.order_ref, bf16[2,2,32,64,2048]{4,3,2,1,0:T(8,128)(2,1)} %wigner_ref.7, bf16[2,2,64,2048]{3,2,1,0:T(8,128)(2,1)S(1)} %broadcast_select_fusion.1.sky_ref, bf16[16,8,128,128]{3,2,1,0:T(8,128)(2,1)} %bitcast.16), custom_call_target="tpu_custom_call" | custom-call | flops 4000000000 | bytes 20000000 | tf_op jit(solution)/shard_map/spin_1/pallas_call | solution.py:177
  203.6 0.0 copy-start.2
  203.6 1.3 copy-done.2
  204.9 10.7 %spin_2.1 = f32[2,2,8,128,128]{4,3,2,1,0:T(8,128)S(1)} custom-call(s32[2]{0:T(128)S(1)} %get-tuple-element.10.order_ref, bf16[2,2,32,64,2048]{4,3,2,1,0:T(8,128)(2,1)} %wigner_ref.7, bf16[2,2,64,2048]{3,2,1,0:T(8,128)(2,1)S(1)} %broadcast_select_fusion.1.sky_ref, bf16[16,8,128,128]{3,2,1,0:T(8,128)(2,1)} %bitcast.17), custom_call_target="tpu_custom_call" | custom-call | flops 4000000000 | bytes 20000000 | tf_op jit(solution)/shard_map/spin_2/pallas_call | solution.py:177
  215.6 0.0 copy-start
  215.6 1.4 copy-done
  217.0 10.3 %all-gather.9.cloned.1.call-done = bf16[128,128,128]{1,0,2:T(8,128)(2,1)} async-done(((bf16[8,128,128]{1,0,2:T(8,128)(2,1)}), bf16[128,128,128]{1,0,2:T(8,128)(2,1)}) %all-gather.9.cloned.1.call-update) | async-done | bytes 4194320 | tf_op jit(solution)/shard_map/all_gather | solution.py:152
  227.3 6.9 %copy.8 = bf16[128,128,128]{2,1,0:T(8,128)(2,1)} copy(bf16[128,128,128]{1,0,2:T(8,128)(2,1)} %all-gather.9.cloned.1.call-done) | data formatting | bytes 8388608 | tf_op jit(solution)/shard_map/all_gather | solution.py:152
  234.2 0.0 copy-start.5
  234.2 10.8 %spin_3.1 = f32[2,2,8,128,128]{4,3,2,1,0:T(8,128)S(1)} custom-call(s32[2]{0:T(128)S(1)} %get-tuple-element.10.order_ref, bf16[2,2,32,64,2048]{4,3,2,1,0:T(8,128)(2,1)} %wigner_ref.7, bf16[2,2,64,2048]{3,2,1,0:T(8,128)(2,1)S(1)} %broadcast_select_fusion.1.sky_ref, bf16[16,8,128,128]{3,2,1,0:T(8,128)(2,1)} %bitcast.18), custom_call_target="tpu_custom_call" | custom-call | flops 4000000000 | bytes 20000000 | tf_op jit(solution)/shard_map/spin_3/pallas_call | solution.py:177
  245.1 0.0 copy-done.5
  245.1 0.0 copy-start.3
  245.1 23.2 %stream_0.1.before_ref = f32[128,1024]{1,0:T(8,128)S(1)} custom-call(s32[2]{0:T(128)S(1)} %get-tuple-element.10.order_ref, f32[2,2048,128]{2,1,0:T(8,128)S(1)} %bitcast.14, bf16[128,128,1024]{2,1,0:T(8,128)(2,1)} %get-tuple-element.7.phase_ref, f32[128,16,1024]{2,1,0:T(8,128)} %get-tuple-element.8.orient_ref, s32[128,1024]{1,0:T(8,128)S(1)} %all_gather.29.pointing_ref, ...), custom_call_target="tpu_custom_call" | custom-call | flops 6000000000 | bytes 40000000 | tf_op jit(solution)/shard_map/stream_0/pallas_call | solution.py:209
  268.3 0.0 copy-done.3
  268.3 0.0 copy-start.1
  268.3 23.3 %stream_1.1.before_ref = f32[128,1024]{1,0:T(8,128)S(1)} custom-call(s32[2]{0:T(128)S(1)} %get-tuple-element.10.order_ref, f32[2,2048,128]{2,1,0:T(8,128)S(1)} %bitcast.12, bf16[128,128,1024]{2,1,0:T(8,128)(2,1)} %get-tuple-element.7.phase_ref, f32[128,16,1024]{2,1,0:T(8,128)} %get-tuple-element.8.orient_ref, s32[128,1024]{1,0:T(8,128)S(1)} %all_gather.29.pointing_ref, ...), custom_call_target="tpu_custom_call" | custom-call | flops 6000000000 | bytes 40000000 | tf_op jit(solution)/shard_map/stream_1/pallas_call | solution.py:209
  291.6 0.0 copy-done.1
  291.6 23.2 %stream_2.1.before_ref = f32[128,1024]{1,0:T(8,128)S(1)} custom-call(s32[2]{0:T(128)S(1)} %get-tuple-element.10.order_ref, f32[2,2048,128]{2,1,0:T(8,128)S(1)} %bitcast.11, bf16[128,128,1024]{2,1,0:T(8,128)(2,1)} %get-tuple-element.7.phase_ref, f32[128,16,1024]{2,1,0:T(8,128)} %get-tuple-element.8.orient_ref, s32[128,1024]{1,0:T(8,128)S(1)} %all_gather.29.pointing_ref, ...), custom_call_target="tpu_custom_call" | custom-call | flops 6000000000 | bytes 40000000 | tf_op jit(solution)/shard_map/stream_2/pallas_call | solution.py:209
  314.8 23.8 %stream_3.1 = f32[128,1024]{1,0:T(8,128)} custom-call(s32[2]{0:T(128)S(1)} %get-tuple-element.10.order_ref, f32[2,2048,128]{2,1,0:T(8,128)S(1)} %bitcast.13, bf16[128,128,1024]{2,1,0:T(8,128)(2,1)} %get-tuple-element.7.phase_ref, f32[128,16,1024]{2,1,0:T(8,128)} %get-tuple-element.8.orient_ref, s32[128,1024]{1,0:T(8,128)S(1)} %all_gather.29.pointing_ref, ...), custom_call_target="tpu_custom_call" | custom-call | flops 6000000000 | bytes 40000000 | tf_op jit(solution)/shard_map/stream_3/pallas_call | solution.py:209
  338.6 0.0 reduce-scatter.2.cloned.1.call-update
  338.7 54.0 %reduce-scatter.2.cloned.1.call-done = f32[8,1024]{1,0:T(8,128)} async-done(((f32[128,1024]{1,0:T(8,128)}), f32[8,1024]{1,0:T(8,128)}) %reduce-scatter.2.cloned.1.call-update) | async-done | bytes 32784 | tf_op jit(solution)/shard_map/reduce_scatter | solution.py:231
  (3 shorter events, 0.1 us)
Async XLA Ops:
  6.5 5.0 %copy-start.8 = (s32[32]{0:T(128)S(1)}, s32[32]{0:T(128)}, u32[]{:S(2)}) copy-start(s32[32]{0:T(128)} %param.8) | copy-start | bytes 388
  6.5 5.2 %copy-start.7 = (s32[8,1024]{1,0:T(8,128)S(1)}, s32[8,1024]{1,0:T(8,128)}, u32[]{:S(2)}) copy-start(s32[8,1024]{1,0:T(8,128)} %param.9) | copy-start | bytes 98308
  6.5 31.0 %copy-start.6 = (bf16[2,2,64,2048]{3,2,1,0:T(8,128)(2,1)S(1)}, bf16[2,2,64,2048]{3,2,1,0:T(8,128)(2,1)}, u32[]{:S(2)}) copy-start(bf16[2,2,64,2048]{3,2,1,0:T(8,128)(2,1)} %param.6) | copy-start | bytes 3145732
  6.5 61.7 %all-gather.15.cloned.1.call-start = ((), (), s32[]{:S(2)}) async-start(), calls=%async_computation.5 | async-start | bytes 4456448 | tf_op jit(solution)/shard_map/all_gather | solution.py:152
  9.4 110.8 %all-gather.13.cloned.1.call-start = ((), (), s32[]{:S(2)}) async-start(), calls=%async_computation.4 | async-start | bytes 4456448 | tf_op jit(solution)/shard_map/all_gather | solution.py:152
  10.2 163.6 %all-gather.11.cloned.1.call-start = ((), (), s32[]{:S(2)}) async-start(), calls=%async_computation.3 | async-start | bytes 4456448 | tf_op jit(solution)/shard_map/all_gather | solution.py:152
  10.9 216.4 %all-gather.9.cloned.1.call-start = ((), (), s32[]{:S(2)}) async-start(), calls=%async_computation.2 | async-start | bytes 4456448 | tf_op jit(solution)/shard_map/all_gather | solution.py:152
  11.5 381.1 %reduce-scatter.2.cloned.1.call-start = ((), (), s32[]{:S(2)}) async-start(), calls=%async_computation.1 | async-start | bytes 557056 | tf_op jit(solution)/shard_map/reduce_scatter | solution.py:231
  191.4 1.4 copy-start.4
  203.6 1.3 copy-start.2
  215.6 1.4 copy-start
  234.2 10.9 %copy-start.5 = (f32[2,2,8,128,128]{4,3,2,1,0:T(8,128)S(1)}, f32[2,2,8,128,128]{4,3,2,1,0:T(8,128)}, u32[]{:S(2)}) copy-start(f32[2,2,8,128,128]{4,3,2,1,0:T(8,128)} %copy-done.4) | copy-start | bytes 6291460
  245.1 23.2 %copy-start.3 = (f32[2,2,8,128,128]{4,3,2,1,0:T(8,128)S(1)}, f32[2,2,8,128,128]{4,3,2,1,0:T(8,128)}, u32[]{:S(2)}) copy-start(f32[2,2,8,128,128]{4,3,2,1,0:T(8,128)} %copy-done.2) | copy-start | bytes 6291460
  268.3 23.3 %copy-start.1 = (f32[2,2,8,128,128]{4,3,2,1,0:T(8,128)S(1)}, f32[2,2,8,128,128]{4,3,2,1,0:T(8,128)}, u32[]{:S(2)}) copy-start(f32[2,2,8,128,128]{4,3,2,1,0:T(8,128)} %copy-done) | copy-start | bytes 6291460
Sparse Core Ops, SparseCore 0:
  9.6 57.0 all-gather.14
  68.8 51.3 all-gather.12
  122.3 51.3 all-gather.10
  175.8 51.4 all-gather.8
  338.8 53.8 reduce-scatter.1

commit v2 on v1

--- a/solution.py
+++ b/solution.py
@@ -8,7 +8,6 @@
 from jax.experimental.pallas import tpu as pltpu
 from jax.sharding import PartitionSpec as P
 
-CHUNKS = 4
 ROWS = 8
 VMEM_LIMIT = 48 * 1024 * 1024
 
@@ -89,18 +88,25 @@
             out_ref[r, b, 0] = both.T
 
 
-def stream_kernel(first_k, spins, cycle_pixels, orient_bins, detectors, block_size, order_ref,
-                  spin_ref, phase_ref, orient_ref, pointing_ref, before_ref, out_ref):
+def stream_kernel(chunks, cycle_pixels, orient_bins, detectors, block_size, order_ref, *refs):
+    spin_refs = refs[: len(chunks)]
+    phase_ref, orient_ref, pointing_ref, out_ref = refs[len(chunks) :]
     samples = pointing_ref.shape[1]
     blocks = order_ref.shape[0]
     step = cycle_pixels // orient_bins
-    groups = spins // ROWS
     first = pl.program_id(1) * pointing_ref.shape[0]
-    row_id = lax.broadcasted_iota(jnp.int32, (max(ROWS, blocks * groups), samples), 0)
-    k_outer = (first_k + (row_id % groups) * ROWS) * step
+    outer = [
+        (b, first_k + a * ROWS)
+        for first_k, size in chunks
+        for b in range(blocks)
+        for a in range(size // ROWS)
+    ]
+    row_id = lax.broadcasted_iota(jnp.int32, (max(ROWS, len(outer)), samples), 0)
+    k_outer = jnp.zeros_like(row_id)
     m_outer = jnp.zeros_like(row_id)
-    for b in range(blocks):
-        m_outer = jnp.where(row_id // groups == b, order_ref[b] * block_size, m_outer)
+    for g, (b, k) in enumerate(outer):
+        k_outer = jnp.where(row_id == g, k * step, k_outer)
+        m_outer = jnp.where(row_id == g, order_ref[b] * block_size, m_outer)
     for j in range(pointing_ref.shape[0]):
         point = pointing_ref[pl.ds(j, 1), :]
         pixel = point // orient_bins
@@ -108,20 +114,25 @@
         outer_cos, outer_sin = sincos(k_outer * orient + m_outer * pixel, cycle_pixels)
         base_cos = orient_ref[j, :ROWS]
         base_sin = orient_ref[j, ROWS:]
-        count = blocks * spins
-        real_rows = spin_ref[0, pl.ds(first + j, count, stride=2 * detectors), :]
-        imag_rows = spin_ref[0, pl.ds(first + j + detectors, count, stride=2 * detectors), :]
-        rows = jnp.concatenate([real_rows, imag_rows], axis=0).astype(jnp.bfloat16)
+        pieces = []
+        for part in range(2):
+            for (_, size), spin_ref in zip(chunks, spin_refs):
+                start = first + j + part * detectors
+                pieces.append(
+                    spin_ref[0, pl.ds(start, blocks * size, stride=2 * detectors), :]
+                )
+        rows = jnp.concatenate(pieces, axis=0).astype(jnp.bfloat16)
         cycle = jnp.dot(rows, phase_ref[j], preferred_element_type=jnp.float32)
+        imag_at = rows.shape[0] // 2
         total = jnp.zeros((ROWS, samples), jnp.float32)
-        for g in range(blocks * groups):
+        for g in range(len(outer)):
             oc = outer_cos[g : g + 1]
             os = outer_sin[g : g + 1]
             real = cycle[g * ROWS : (g + 1) * ROWS]
-            imag = cycle[count + g * ROWS : count + (g + 1) * ROWS]
-            total += real * (oc * base_cos - os * base_sin)
-            total -= imag * (os * base_cos + oc * base_sin)
-        out_ref[pl.ds(j, 1), :] = before_ref[pl.ds(j, 1), :] + jnp.sum(total, axis=0, keepdims=True)
+            imag = cycle[imag_at + g * ROWS : imag_at + (g + 1) * ROWS]
+            total += oc * (real * base_cos - imag * base_sin)
+            total -= os * (real * base_sin + imag * base_cos)
+        out_ref[pl.ds(j, 1), :] = jnp.sum(total, axis=0, keepdims=True)
 
 
 def body(wigner, sky_blocks, beam, block_order, pointing):
@@ -134,7 +145,8 @@
     orient_bins = 4 * spins
     pairs = cycles * detectors
     samples = pointing.shape[1]
-    chunk = spins // CHUNKS
+    last = spins // 4
+    chunks = [(0, spins - last), (spins - last, last)]
     params = pltpu.CompilerParams(vmem_limit_bytes=VMEM_LIMIT)
 
     degree = jnp.arange(degrees, dtype=jnp.int32)
@@ -148,10 +160,13 @@
     k_index = jnp.arange(spins, dtype=jnp.int32)
     turned = jnp.where(here[None, :, None] >= k_index[:, None, None], turned, jnp.bfloat16(0))
 
-    gathered = [
-        lax.all_gather(turned[c * chunk : (c + 1) * chunk], "sky", axis=0, tiled=False)
-        for c in range(CHUNKS)
-    ]
+    gathered = []
+    for first_k, size in chunks:
+        piece = turned[first_k : first_k + size].reshape(size * degrees_here, lanes)
+        if gathered:
+            piece, gathered[-1] = lax.optimization_barrier((piece, gathered[-1]))
+        whole = lax.all_gather(piece, "sky", axis=0, tiled=True)
+        gathered.append(whole.reshape(degrees // degrees_here, size, degrees_here, lanes))
 
     phases, orients = pl.pallas_call(
         functools.partial(phase_kernel, cycle_pixels, orient_bins),
@@ -170,65 +185,70 @@
         name="phases",
     )(points)
 
-    count = blocks * chunk * lanes
-    stream = jnp.zeros((pairs, samples), jnp.float32)
-    for c in range(CHUNKS):
-        first_k = c * chunk
-        spin_sums = pl.pallas_call(
-            functools.partial(spin_kernel, first_k),
-            grid=(chunk,),
-            in_specs=[
-                pl.BlockSpec(memory_space=pltpu.SMEM),
-                pl.BlockSpec(
-                    (blocks, cycles, 1, block_size, degrees),
-                    lambda k, first_k=first_k: (0, 0, first_k + k, 0, 0),
+    spin_parts = []
+    for c, (first_k, size) in enumerate(chunks):
+        spin_parts.append(
+            pl.pallas_call(
+                functools.partial(spin_kernel, first_k),
+                grid=(size,),
+                in_specs=[
+                    pl.BlockSpec(memory_space=pltpu.SMEM),
+                    pl.BlockSpec(
+                        (blocks, cycles, 1, block_size, degrees),
+                        lambda k, first_k=first_k: (0, 0, first_k + k, 0, 0),
+                    ),
+                    pl.BlockSpec((blocks, 2, block_size, degrees), lambda k: (0, 0, 0, 0)),
+                    pl.BlockSpec(
+                        (degrees // degrees_here, 1, degrees_here, lanes),
+                        lambda k: (0, k, 0, 0),
+                    ),
+                ],
+                out_specs=pl.BlockSpec(
+                    (cycles, blocks, 1, lanes, 2 * block_size), lambda k: (0, 0, k, 0, 0)
                 ),
-                pl.BlockSpec((blocks, 2, block_size, degrees), lambda k: (0, 0, 0, 0)),
-                pl.BlockSpec(
-                    (degrees // degrees_here, 1, degrees_here, lanes), lambda k: (0, k, 0, 0)
+                out_shape=jax.ShapeDtypeStruct(
+                    (cycles, blocks, size, lanes, 2 * block_size), jnp.float32
                 ),
-            ],
-            out_specs=pl.BlockSpec(
-                (cycles, blocks, 1, lanes, 2 * block_size), lambda k: (0, 0, k, 0, 0)
-            ),
-            out_shape=jax.ShapeDtypeStruct(
-                (cycles, blocks, chunk, lanes, 2 * block_size), jnp.float32
-            ),
-            scratch_shapes=[
-                pltpu.VMEM((2 * blocks * cycles * block_size, degrees), jnp.bfloat16)
-            ],
-            compiler_params=params,
-            cost_estimate=pl.CostEstimate(
-                flops=4 * 10**9, bytes_accessed=2 * 10**7, transcendentals=0
-            ),
-            name=f"spin_{c}",
-        )(own_blocks, wigner, sky, gathered[c])
-        spin_sums = spin_sums.reshape(cycles, count, 2 * block_size)
-        row_of = lambda r, e: (r * (detectors // ROWS) + e, 0)
-        pair_of = lambda r, e: (r * (detectors // ROWS) + e, 0, 0)
-        stream = pl.pallas_call(
-            functools.partial(
-                stream_kernel, first_k, chunk, cycle_pixels, orient_bins, detectors, block_size
-            ),
-            grid=(cycles, detectors // ROWS),
-            in_specs=[
-                pl.BlockSpec(memory_space=pltpu.SMEM),
-                pl.BlockSpec((1, count, 2 * block_size), lambda r, e: (r, 0, 0)),
-                pl.BlockSpec((ROWS, 2 * block_size, samples), pair_of),
-                pl.BlockSpec((ROWS, 2 * ROWS, samples), pair_of),
-                pl.BlockSpec((ROWS, samples), row_of),
-                pl.BlockSpec((ROWS, samples), row_of),
-            ],
-            out_specs=pl.BlockSpec((ROWS, samples), row_of),
-            out_shape=jax.ShapeDtypeStruct((pairs, samples), jnp.float32),
-            compiler_params=params,
-            cost_estimate=pl.CostEstimate(
-                flops=6 * 10**9, bytes_accessed=4 * 10**7, transcendentals=0
-            ),
-            name=f"stream_{c}",
-        )(own_blocks, spin_sums, phases, orients, points, stream)
-
-    return lax.psum_scatter(stream, "sky", scatter_dimension=0, tiled=True)
+                scratch_shapes=[
+                    pltpu.VMEM((2 * blocks * cycles * block_size, degrees), jnp.bfloat16)
+                ],
+                compiler_params=params,
+                cost_estimate=pl.CostEstimate(
+                    flops=10**9 * size, bytes_accessed=2 * 10**6 * size, transcendentals=0
+                ),
+                name=f"spin_{c}",
+            )(own_blocks, wigner, sky, gathered[c]).reshape(
+                cycles, blocks * size * lanes, 2 * block_size
+            )
+        )
+    row_of = lambda r, e: (r * (detectors // ROWS) + e, 0)
+    pair_of = lambda r, e: (r * (detectors // ROWS) + e, 0, 0)
+    stream = pl.pallas_call(
+        functools.partial(
+            stream_kernel, chunks, cycle_pixels, orient_bins, detectors, block_size
+        ),
+        grid=(cycles, detectors // ROWS),
+        in_specs=[pl.BlockSpec(memory_space=pltpu.SMEM)]
+        + [
+            pl.BlockSpec((1,) + part.shape[1:], lambda r, e: (r, 0, 0)) for part in spin_parts
+        ]
+        + [
+            pl.BlockSpec((ROWS, 2 * block_size, samples), pair_of),
+            pl.BlockSpec((ROWS, 2 * ROWS, samples), pair_of),
+            pl.BlockSpec((ROWS, samples), row_of),
+        ],
+        out_specs=pl.BlockSpec((ROWS, samples), row_of),
+        out_shape=jax.ShapeDtypeStruct((pairs, samples), jnp.float32),
+        compiler_params=params,
+        cost_estimate=pl.CostEstimate(flops=2 * 10**10, bytes_accessed=5 * 10**7, transcendentals=0),
+        name="stream",
+    )(own_blocks, *spin_parts, phases, orients, points)
+
+    owners = pairs // pointing.shape[0]
+    parts = lax.all_to_all(
+        stream.reshape(owners, pointing.shape[0], samples), "sky", split_axis=0, concat_axis=0
+    )
+    return jnp.sum(parts, axis=0)
 
 
 def solution(mesh):

time: 402 us -> 269 us (0.67)
  Pallas kernels: 167 us -> 108 us
  waiting for transfers between devices: 158 us -> 104 us
  local copies, waits for them, and re-layouts: 34.4 us -> 4.08 us
  blocking collectives: 25.6 us -> 37.6 us
    pallas_call x8 -> x3, Pallas kernels: 137 us -> 77.3 us  [the longest x2 42.2 us: body(): pl.pallas_call(functools.partial(spin_kernel, first_k), grid=(size,), in_...]
    reduce_scatter x1 -> x0, waiting for transfers between devices: 54 us -> none  [body(): return lax.psum_scatter(stream, 'sky', scatter_dimension=0, tiled=True)]
    all_gather x4 -> x0, local copies, waits for them, and re-layouts: 27.6 us -> none  [body(): lax.all_gather(turned[c * chunk:(c + 1) * chunk], 'sky', axis=0, tiled=Fa...]
    all_to_all x0 -> x1, blocking collectives: none -> 17.1 us  [body(): lax.all_to_all(stream.reshape(owners, pointing.shape[0], samples), 'sky',...]
    all_gather x1, blocking collectives: 25.6 us -> 20.5 us  [body(): points = lax.all_gather(pointing, 'sky', axis=0, tiled=True)]
    all_gather x4 -> x2, waiting for transfers between devices: 102 us -> 103 us  [body(): whole = lax.all_gather(piece, 'sky', axis=0, tiled=True)]
  transfers between devices with their start and end apart: 5 -> 2, of which waited for: 4 -> 1; matrix products, arithmetic and copies ran while one was open for 5% -> 0% of each run, Pallas kernels for 16% -> 23%
where the time goes in v2:
time: 269 us; the launch traced here: 268 us
  Pallas kernels  108 us (40%)
  waiting for transfers between devices  104 us (39%)
  blocking collectives  37.6 us (14%)
  between operations  13.5 us (5%)
  local copies, waits for them, and re-layouts  4.08 us (2%)
    all_gather x2, waiting for transfers between devices, body(): whole = lax.all_gather(piece, 'sky', axis=0, tiled=True)  103 us
    pallas_call x2, Pallas kernels, body(): pl.pallas_call(functools.partial(spin_kernel, first_k), grid=(size,), in_...  42.2 us
    pallas_call x1, Pallas kernels, body(): pl.pallas_call(functools.partial(stream_kernel, chunks, cycle_pixels, ori...  35 us
    pallas_call x1, Pallas kernels, body(): pl.pallas_call(functools.partial(phase_kernel, cycle_pixels, orient_bins)...  30.7 us
    all_gather x1, blocking collectives, body(): points = lax.all_gather(pointing, 'sky', axis=0, tiled=True)  20.5 us
    all_to_all x1, blocking collectives, body(): lax.all_to_all(stream.reshape(owners, pointing.shape[0], samples), 'sky',...  17.1 us
  transfers between devices with their start and end apart: 2, of which 1 were waited for; matrix products, arithmetic and copies ran while one was open for 0% of the time, Pallas kernels for 23%

profile of v2, /device:TPU:0, one launch (start us, length us, event | category | flops | bytes accessed | tf_op | source)
XLA Modules:
  0.0 267.9 jit_solution(7887709132761165761)
XLA Ops:
  6.5 0.0 copy-start.2
  6.5 0.0 copy-start.1
  6.5 0.0 copy-start
  6.5 0.0 all-gather.3.cloned.1.call-start
  6.6 1.7 copy.8
  8.3 0.1 broadcast_select_fusion
  8.4 0.1 slice.9
  8.4 1.4 copy.11
  9.8 0.0 all-gather.3.cloned.1.call-update
  9.8 0.0 all-gather.5.cloned.1.call-start
  10.0 103.5 %all-gather.3.cloned.1.call-done = bf16[49152,128]{1,0:T(8,128)(2,1)} async-done(((bf16[3072,128]{1,0:T(8,128)(2,1)}), bf16[49152,128]{1,0:T(8,128)(2,1)}) %all-gather.3.cloned.1.call-update) | async-done | bytes 12582928 | tf_op jit(solution)/shard_map/all_gather | solution.py:168
  113.4 0.9 copy.10
  114.3 0.0 all-gather.5.cloned.1.call-update
  114.3 0.0 copy-done.2
  114.3 0.1 broadcast_multiply_fusion
  114.4 0.1 iota_add_fusion
  114.5 0.0 copy-done.1
  114.5 20.5 %all_gather.11.pointing_ref.refs_4_ = s32[128,1024]{1,0:T(8,128)S(1)} all-gather(s32[8,1024]{1,0:T(8,128)S(1)} %copy-done.1), channel_id=1, replica_groups=mesh['groups'=2,'sky'=16] {'sky'}, dimensions={0}, use_global_device_ids=true | all-gather | bytes 557056 | tf_op jit(solution)/shard_map/all_gather | solution.py:157
  135.0 0.2 iota_compare_fusion
  135.2 0.0 copy-done
  135.2 0.1 broadcast_select_fusion.1.sky_ref
  135.3 30.7 %phases.1 = (bf16[128,128,1024]{2,1,0:T(8,128)(2,1)}, f32[128,16,1024]{2,1,0:T(8,128)}) custom-call(s32[128,1024]{1,0:T(8,128)S(1)} %all_gather.11.pointing_ref.refs_4_), custom_call_target="tpu_custom_call" | custom-call | flops 10000000000 | bytes 50000000 | tf_op jit(solution)/shard_map/phases/pallas_call | solution.py:171
  166.0 31.6 %spin_0.1 = f32[2,2,24,128,128]{4,3,2,1,0:T(8,128)} custom-call(s32[2]{0:T(128)S(1)} %get-tuple-element.14.order_ref, bf16[2,2,32,64,2048]{4,3,2,1,0:T(8,128)(2,1)} %wigner_ref.3, bf16[2,2,64,2048]{3,2,1,0:T(8,128)(2,1)S(1)} %broadcast_select_fusion.1.sky_ref, bf16[16,24,128,128]{3,2,1,0:T(8,128)(2,1)} %bitcast.22), custom_call_target="tpu_custom_call" | custom-call | flops 24000000000 | bytes 48000000 | tf_op jit(solution)/shard_map/spin_0/pallas_call | solution.py:191
  197.6 0.0 all-gather.5.cloned.1.call-done
  197.6 10.7 %spin_1.1 = f32[2,2,8,128,128]{4,3,2,1,0:T(8,128)S(1)} custom-call(s32[2]{0:T(128)S(1)} %get-tuple-element.14.order_ref, bf16[2,2,32,64,2048]{4,3,2,1,0:T(8,128)(2,1)} %wigner_ref.3, bf16[2,2,64,2048]{3,2,1,0:T(8,128)(2,1)S(1)} %broadcast_select_fusion.1.sky_ref, bf16[16,8,128,128]{3,2,1,0:T(8,128)(2,1)} %bitcast.18), custom_call_target="tpu_custom_call" | custom-call | flops 8000000000 | bytes 16000000 | tf_op jit(solution)/shard_map/spin_1/pallas_call | solution.py:191
  208.3 35.0 %stream.1 = f32[128,1024]{1,0:T(8,128)S(1)} custom-call(s32[2]{0:T(128)S(1)} %get-tuple-element.14.order_ref, f32[2,6144,128]{2,1,0:T(8,128)} %bitcast.23, f32[2,2048,128]{2,1,0:T(8,128)S(1)} %bitcast.15, bf16[128,128,1024]{2,1,0:T(8,128)(2,1)} %get-tuple-element.11.refs_2_, f32[128,16,1024]{2,1,0:T(8,128)} %get-tuple-element.12.refs_3_, ...), custom_call_target="tpu_custom_call" | custom-call | flops 20000000000 | bytes 50000000 | tf_op jit(solution)/shard_map/stream/pallas_call | solution.py:226
  243.3 17.1 %all_to_all.5 = f32[16,8,1024]{2,1,0:T(8,128)S(1)} all-to-all(f32[16,8,1024]{2,1,0:T(8,128)S(1)} %bitcast.16), channel_id=1, replica_groups=mesh['groups'=2,'sky'=16] {'sky'}, dimensions={0} | all-to-all | bytes 1048576 | tf_op jit(solution)/shard_map/all_to_all | solution.py:248
  260.4 0.6 reduce_sum.9
  (4 shorter events, 0.1 us)
Async XLA Ops:
  6.5 107.8 %copy-start.2 = (s32[32]{0:T(128)S(1)}, s32[32]{0:T(128)}, u32[]{:S(2)}) copy-start(s32[32]{0:T(128)} %param.8) | copy-start | bytes 388
  6.5 107.9 %copy-start.1 = (s32[8,1024]{1,0:T(8,128)S(1)}, s32[8,1024]{1,0:T(8,128)}, u32[]{:S(2)}) copy-start(s32[8,1024]{1,0:T(8,128)} %param.9) | copy-start | bytes 98308
  6.5 128.7 %copy-start = (bf16[2,2,64,2048]{3,2,1,0:T(8,128)(2,1)S(1)}, bf16[2,2,64,2048]{3,2,1,0:T(8,128)(2,1)}, u32[]{:S(2)}) copy-start(bf16[2,2,64,2048]{3,2,1,0:T(8,128)(2,1)} %param.6) | copy-start | bytes 3145732
  6.5 106.9 %all-gather.3.cloned.1.call-start = ((), (), s32[]{:S(2)}) async-start(), calls=%async_computation.1 | async-start | bytes 13369344 | tf_op jit(solution)/shard_map/all_gather | solution.py:168
  9.8 187.8 %all-gather.5.cloned.1.call-start = ((), (), s32[]{:S(2)}) async-start(), calls=%async_computation.2 | async-start | bytes 4456448 | tf_op jit(solution)/shard_map/all_gather | solution.py:168
Sparse Core Ops, SparseCore 0:
  9.9 103.4 all-gather.2
  115.6 50.1 all-gather.4

commit v3 on v2

--- a/solution.py
+++ b/solution.py
@@ -30,11 +30,21 @@
     return cos_value, sin_value
 
 
-def phase_kernel(cycle_pixels, orient_bins, pointing_ref, phase_ref, orient_ref):
+def phase_kernel(
+    cycle_pixels, orient_bins, spins, order_ref, pointing_ref, phase_ref, orient_ref
+):
     samples = pointing_ref.shape[1]
     block_size = phase_ref.shape[1] // 2
     step = cycle_pixels // orient_bins
     low = lax.broadcasted_iota(jnp.int32, (ROWS, samples), 0)
+    blocks = order_ref.shape[0]
+    groups = spins // ROWS
+    row_id = lax.broadcasted_iota(jnp.int32, (blocks * groups, samples), 0)
+    k_outer = (row_id & (groups - 1)) * ROWS * step
+    m_outer = jnp.zeros_like(row_id)
+    for b in range(blocks):
+        inside = (row_id >= b * groups) & (row_id < (b + 1) * groups)
+        m_outer = jnp.where(inside, order_ref[b] * block_size, m_outer)
     for j in range(pointing_ref.shape[0]):
         point = pointing_ref[pl.ds(j, 1), :]
         pixel = jnp.broadcast_to(point // orient_bins, (ROWS, samples))
@@ -54,7 +64,9 @@
                 sin_rows.append(os * base_cos + oc * base_sin)
         phase_ref[j] = jnp.concatenate(cos_rows + sin_rows, axis=0).astype(jnp.bfloat16)
         orient_cos, orient_sin = sincos(low * orient * step, cycle_pixels)
-        orient_ref[j] = jnp.concatenate([orient_cos, orient_sin], axis=0)
+        turns = k_outer * (point & (orient_bins - 1)) + m_outer * (point // orient_bins)
+        outer_cos, outer_sin = sincos(turns, cycle_pixels)
+        orient_ref[j] = jnp.concatenate([orient_cos, orient_sin, outer_cos, outer_sin], axis=0)
 
 
 def spin_kernel(first_k, order_ref, wigner_ref, sky_ref, beam_ref, out_ref, coeff):
@@ -88,48 +100,33 @@
             out_ref[r, b, 0] = both.T
 
 
-def stream_kernel(chunks, cycle_pixels, orient_bins, detectors, block_size, order_ref, *refs):
+def stream_kernel(chunks, detectors, blocks, *refs):
     spin_refs = refs[: len(chunks)]
-    phase_ref, orient_ref, pointing_ref, out_ref = refs[len(chunks) :]
-    samples = pointing_ref.shape[1]
-    blocks = order_ref.shape[0]
-    step = cycle_pixels // orient_bins
-    first = pl.program_id(1) * pointing_ref.shape[0]
-    outer = [
-        (b, first_k + a * ROWS)
-        for first_k, size in chunks
-        for b in range(blocks)
-        for a in range(size // ROWS)
-    ]
-    row_id = lax.broadcasted_iota(jnp.int32, (max(ROWS, len(outer)), samples), 0)
-    k_outer = jnp.zeros_like(row_id)
-    m_outer = jnp.zeros_like(row_id)
-    for g, (b, k) in enumerate(outer):
-        k_outer = jnp.where(row_id == g, k * step, k_outer)
-        m_outer = jnp.where(row_id == g, order_ref[b] * block_size, m_outer)
-    for j in range(pointing_ref.shape[0]):
-        point = pointing_ref[pl.ds(j, 1), :]
-        pixel = point // orient_bins
-        orient = point & (orient_bins - 1)
-        outer_cos, outer_sin = sincos(k_outer * orient + m_outer * pixel, cycle_pixels)
+    phase_ref, orient_ref, out_ref, rows = refs[len(chunks) :]
+    samples = out_ref.shape[1]
+    spins = sum(size for _, size in chunks)
+    count = blocks * spins
+    outer = count // ROWS
+    first = pl.program_id(1) * ROWS
+    for j in range(ROWS):
+        for part in range(2):
+            start = first + j + part * detectors
+            for (first_k, size), spin_ref in zip(chunks, spin_refs):
+                for b in range(blocks):
+                    rows[j % 2, pl.ds(part * count + b * spins + first_k, size), :] = spin_ref[
+                        0, pl.ds(b * size * 2 * detectors + start, size, stride=2 * detectors), :
+                    ]
+        cycle = jnp.dot(
+            rows[j % 2].astype(jnp.bfloat16), phase_ref[j], preferred_element_type=jnp.float32
+        )
         base_cos = orient_ref[j, :ROWS]
-        base_sin = orient_ref[j, ROWS:]
-        pieces = []
-        for part in range(2):
-            for (_, size), spin_ref in zip(chunks, spin_refs):
-                start = first + j + part * detectors
-                pieces.append(
-                    spin_ref[0, pl.ds(start, blocks * size, stride=2 * detectors), :]
-                )
-        rows = jnp.concatenate(pieces, axis=0).astype(jnp.bfloat16)
-        cycle = jnp.dot(rows, phase_ref[j], preferred_element_type=jnp.float32)
-        imag_at = rows.shape[0] // 2
+        base_sin = orient_ref[j, ROWS : 2 * ROWS]
         total = jnp.zeros((ROWS, samples), jnp.float32)
-        for g in range(len(outer)):
-            oc = outer_cos[g : g + 1]
-            os = outer_sin[g : g + 1]
+        for g in range(outer):
+            oc = orient_ref[j, pl.ds(2 * ROWS + g, 1), :]
+            os = orient_ref[j, pl.ds(2 * ROWS + outer + g, 1), :]
             real = cycle[g * ROWS : (g + 1) * ROWS]
-            imag = cycle[imag_at + g * ROWS : imag_at + (g + 1) * ROWS]
+            imag = cycle[count + g * ROWS : count + (g + 1) * ROWS]
             total += oc * (real * base_cos - imag * base_sin)
             total -= os * (real * base_sin + imag * base_cos)
         out_ref[pl.ds(j, 1), :] = jnp.sum(total, axis=0, keepdims=True)
@@ -145,7 +142,7 @@
     orient_bins = 4 * spins
     pairs = cycles * detectors
     samples = pointing.shape[1]
-    last = spins // 4
+    last = spins // 8
     chunks = [(0, spins - last), (spins - last, last)]
     params = pltpu.CompilerParams(vmem_limit_bytes=VMEM_LIMIT)
 
@@ -160,30 +157,35 @@
     k_index = jnp.arange(spins, dtype=jnp.int32)
     turned = jnp.where(here[None, :, None] >= k_index[:, None, None], turned, jnp.bfloat16(0))
 
+    table_rows = 2 * ROWS + 2 * blocks * (spins // ROWS)
+    phases, orients = pl.pallas_call(
+        functools.partial(phase_kernel, cycle_pixels, orient_bins, spins),
+        grid=(pairs // ROWS,),
+        in_specs=[
+            pl.BlockSpec(memory_space=pltpu.SMEM),
+            pl.BlockSpec((ROWS, samples), lambda p: (p, 0)),
+        ],
+        out_specs=[
+            pl.BlockSpec((ROWS, 2 * block_size, samples), lambda p: (p, 0, 0)),
+            pl.BlockSpec((ROWS, table_rows, samples), lambda p: (p, 0, 0)),
+        ],
+        out_shape=[
+            jax.ShapeDtypeStruct((pairs, 2 * block_size, samples), jnp.bfloat16),
+            jax.ShapeDtypeStruct((pairs, table_rows, samples), jnp.float32),
+        ],
+        compiler_params=params,
+        cost_estimate=pl.CostEstimate(flops=10**10, bytes_accessed=5 * 10**7, transcendentals=0),
+        name="phases",
+    )(own_blocks, points)
+
     gathered = []
     for first_k, size in chunks:
         piece = turned[first_k : first_k + size].reshape(size * degrees_here, lanes)
         if gathered:
+            piece, phases, orients = lax.optimization_barrier((piece, phases, orients))
             piece, gathered[-1] = lax.optimization_barrier((piece, gathered[-1]))
         whole = lax.all_gather(piece, "sky", axis=0, tiled=True)
         gathered.append(whole.reshape(degrees // degrees_here, size, degrees_here, lanes))
-
-    phases, orients = pl.pallas_call(
-        functools.partial(phase_kernel, cycle_pixels, orient_bins),
-        grid=(pairs // ROWS,),
-        in_specs=[pl.BlockSpec((ROWS, samples), lambda p: (p, 0))],
-        out_specs=[
-            pl.BlockSpec((ROWS, 2 * block_size, samples), lambda p: (p, 0, 0)),
-            pl.BlockSpec((ROWS, 2 * ROWS, samples), lambda p: (p, 0, 0)),
-        ],
-        out_shape=[
-            jax.ShapeDtypeStruct((pairs, 2 * block_size, samples), jnp.bfloat16),
-            jax.ShapeDtypeStruct((pairs, 2 * ROWS, samples), jnp.float32),
-        ],
-        compiler_params=params,
-        cost_estimate=pl.CostEstimate(flops=10**10, bytes_accessed=5 * 10**7, transcendentals=0),
-        name="phases",
-    )(points)
 
     spin_parts = []
     for c, (first_k, size) in enumerate(chunks):
@@ -224,25 +226,22 @@
     row_of = lambda r, e: (r * (detectors // ROWS) + e, 0)
     pair_of = lambda r, e: (r * (detectors // ROWS) + e, 0, 0)
     stream = pl.pallas_call(
-        functools.partial(
-            stream_kernel, chunks, cycle_pixels, orient_bins, detectors, block_size
-        ),
+        functools.partial(stream_kernel, chunks, detectors, blocks),
         grid=(cycles, detectors // ROWS),
-        in_specs=[pl.BlockSpec(memory_space=pltpu.SMEM)]
-        + [
+        in_specs=[
             pl.BlockSpec((1,) + part.shape[1:], lambda r, e: (r, 0, 0)) for part in spin_parts
         ]
         + [
             pl.BlockSpec((ROWS, 2 * block_size, samples), pair_of),
-            pl.BlockSpec((ROWS, 2 * ROWS, samples), pair_of),
-            pl.BlockSpec((ROWS, samples), row_of),
+            pl.BlockSpec((ROWS, table_rows, samples), pair_of),
         ],
         out_specs=pl.BlockSpec((ROWS, samples), row_of),
         out_shape=jax.ShapeDtypeStruct((pairs, samples), jnp.float32),
+        scratch_shapes=[pltpu.VMEM((2, 2 * blocks * spins, 2 * block_size), jnp.float32)],
         compiler_params=params,
         cost_estimate=pl.CostEstimate(flops=2 * 10**10, bytes_accessed=5 * 10**7, transcendentals=0),
         name="stream",
-    )(own_blocks, *spin_parts, phases, orients, points)
+    )(*spin_parts, phases, orients)
 
     owners = pairs // pointing.shape[0]
     parts = lax.all_to_all(

time: 269 us -> 235 us (0.87)
  waiting for transfers between devices: 104 us -> 57 us
  blocking collectives: 37.6 us -> 44.1 us
  Pallas kernels: 108 us -> 112 us
    all_gather x2, waiting for transfers between devices: 103 us -> 57 us  [body(): whole = lax.all_gather(piece, 'sky', axis=0, tiled=True)]
    all_gather x1, blocking collectives: 20.5 us -> 26.4 us  [body(): points = lax.all_gather(pointing, 'sky', axis=0, tiled=True)]
    pallas_call x2, Pallas kernels: 65.7 us -> 69.6 us  [the longest x1 37.4 us: body(): pl.pallas_call(functools.partial(phase_kernel, cycle_pixels, orient_bins,...]
  transfers between devices with their start and end apart: 2 -> 2, of which waited for: 1 -> 2; matrix products, arithmetic and copies ran while one was open for 0% -> 1% of each run, Pallas kernels for 23% -> 32%
where the time goes in v3:
time: 235 us; the launch traced here: 234 us
  Pallas kernels  112 us (48%)
  waiting for transfers between devices  57 us (24%)
  blocking collectives  44.1 us (19%)
  between operations  13.5 us (6%)
  local copies, waits for them, and re-layouts  5.72 us (2%)
    all_gather x2, waiting for transfers between devices, body(): whole = lax.all_gather(piece, 'sky', axis=0, tiled=True)  57 us
    pallas_call x2, Pallas kernels, body(): pl.pallas_call(functools.partial(spin_kernel, first_k), grid=(size,), in_...  42.1 us
    pallas_call x1, Pallas kernels, body(): pl.pallas_call(functools.partial(phase_kernel, cycle_pixels, orient_bins,...  37.4 us
    pallas_call x1, Pallas kernels, body(): pl.pallas_call(functools.partial(stream_kernel, chunks, detectors, blocks...  32.2 us
    all_gather x1, blocking collectives, body(): points = lax.all_gather(pointing, 'sky', axis=0, tiled=True)  26.4 us
    all_to_all x1, blocking collectives, body(): lax.all_to_all(stream.reshape(owners, pointing.shape[0], samples), 'sky',...  17.7 us
  transfers between devices with their start and end apart: 2, of which 2 were waited for; matrix products, arithmetic and copies ran while one was open for 1% of the time, Pallas kernels for 32%

profile of v3, /device:TPU:0, one launch (start us, length us, event | category | flops | bytes accessed | tf_op | source)
XLA Modules:
  0.0 234.0 jit_solution(4358979659902419112)
XLA Ops:
  6.5 0.0 all-gather.3.cloned.1.call-start
  6.6 1.6 copy.11
  8.2 0.1 broadcast_select_fusion
  8.3 1.7 copy.12
  9.9 0.0 all-gather.3.cloned.1.call-update
  9.9 0.0 all-gather.5.cloned.1.call-start
  10.0 0.1 slice.8
  10.1 0.7 broadcast_multiply_fusion
  10.8 26.4 %all_gather.9.pointing_ref = s32[128,1024]{1,0:T(8,128)S(1)} all-gather(s32[8,1024]{1,0:T(8,128)} %param.9), channel_id=1, replica_groups=mesh['groups'=2,'sky'=16] {'sky'}, dimensions={0}, use_global_device_ids=true | all-gather | bytes 557056 | tf_op jit(solution)/shard_map/all_gather | solution.py:154
  37.2 0.0 copy-start.1
  37.2 37.4 %phases.1 = (bf16[128,128,1024]{2,1,0:T(8,128)(2,1)}, f32[128,32,1024]{2,1,0:T(8,128)}) custom-call(s32[2]{0:T(128)S(1)} %get-tuple-element.20.order_ref, s32[128,1024]{1,0:T(8,128)S(1)} %all_gather.9.pointing_ref), custom_call_target="tpu_custom_call" | custom-call | flops 10000000000 | bytes 50000000 | tf_op jit(solution)/shard_map/phases/pallas_call | solution.py:161
  74.6 53.0 %all-gather.3.cloned.1.call-done = bf16[57344,128]{1,0:T(8,128)(2,1)} async-done(((bf16[3584,128]{1,0:T(8,128)(2,1)}), bf16[57344,128]{1,0:T(8,128)(2,1)}) %all-gather.3.cloned.1.call-update) | async-done | bytes 14680080 | tf_op jit(solution)/shard_map/all_gather | solution.py:187
  127.7 0.8 copy.13
  128.4 0.0 all-gather.5.cloned.1.call-update
  128.4 0.1 iota_add_fusion
  128.5 0.2 iota_compare_fusion
  128.7 0.0 copy-done.1
  128.8 0.1 broadcast_select_fusion.1.sky_ref
  128.9 36.6 %spin_0.1 = f32[2,2,28,128,128]{4,3,2,1,0:T(8,128)} custom-call(s32[2]{0:T(128)S(1)} %get-tuple-element.20.order_ref, bf16[2,2,32,64,2048]{4,3,2,1,0:T(8,128)(2,1)} %wigner_ref.3, bf16[2,2,64,2048]{3,2,1,0:T(8,128)(2,1)S(1)} %broadcast_select_fusion.1.sky_ref, bf16[16,28,128,128]{3,2,1,0:T(8,128)(2,1)} %bitcast.24), custom_call_target="tpu_custom_call" | custom-call | flops 28000000000 | bytes 56000000 | tf_op jit(solution)/shard_map/spin_0/pallas_call | solution.py:193
  165.5 3.9 %all-gather.5.cloned.1.call-done = bf16[8192,128]{1,0:T(8,128)(2,1)} async-done(((bf16[512,128]{1,0:T(8,128)(2,1)}), bf16[8192,128]{1,0:T(8,128)(2,1)}) %all-gather.5.cloned.1.call-update) | async-done | bytes 2097168 | tf_op jit(solution)/shard_map/all_gather | solution.py:187
  169.4 0.0 copy-start
  169.4 1.6 copy-done
  171.0 5.5 %spin_1.1 = f32[2,2,4,128,128]{4,3,2,1,0:T(8,128)S(1)} custom-call(s32[2]{0:T(128)S(1)} %get-tuple-element.20.order_ref, bf16[2,2,32,64,2048]{4,3,2,1,0:T(8,128)(2,1)} %wigner_ref.3, bf16[2,2,64,2048]{3,2,1,0:T(8,128)(2,1)S(1)} %broadcast_select_fusion.1.sky_ref, bf16[16,4,128,128]{3,2,1,0:T(8,128)(2,1)S(1)} %bitcast.16), custom_call_target="tpu_custom_call" | custom-call | flops 4000000000 | bytes 8000000 | tf_op jit(solution)/shard_map/spin_1/pallas_call | solution.py:193
  176.6 32.2 %stream.1 = f32[128,1024]{1,0:T(8,128)S(1)} custom-call(f32[2,7168,128]{2,1,0:T(8,128)} %bitcast.25, f32[2,1024,128]{2,1,0:T(8,128)S(1)} %bitcast.17, bf16[128,128,1024]{2,1,0:T(8,128)(2,1)} %get-tuple-element.17.refs_2_, f32[128,32,1024]{2,1,0:T(8,128)} %get-tuple-element.18.refs_3_), custom_call_target="tpu_custom_call" | custom-call | flops 20000000000 | bytes 50000000 | tf_op jit(solution)/shard_map/stream/pallas_call | solution.py:228
  208.8 17.7 %all_to_all.5 = f32[16,8,1024]{2,1,0:T(8,128)S(1)} all-to-all(f32[16,8,1024]{2,1,0:T(8,128)S(1)} %bitcast.18), channel_id=1, replica_groups=mesh['groups'=2,'sky'=16] {'sky'}, dimensions={0} | all-to-all | bytes 1048576 | tf_op jit(solution)/shard_map/all_to_all | solution.py:247
  226.5 0.6 reduce_sum.9
  (3 shorter events, 0.0 us)
Async XLA Ops:
  6.5 121.1 %all-gather.3.cloned.1.call-start = ((), (), s32[]{:S(2)}) async-start(), calls=%async_computation.1 | async-start | bytes 15597568 | tf_op jit(solution)/shard_map/all_gather | solution.py:187
  9.9 159.5 %all-gather.5.cloned.1.call-start = ((), (), s32[]{:S(2)}) async-start(), calls=%async_computation.2 | async-start | bytes 2228224 | tf_op jit(solution)/shard_map/all_gather | solution.py:187
  37.2 91.5 %copy-start.1 = (bf16[2,2,64,2048]{3,2,1,0:T(8,128)(2,1)S(1)}, bf16[2,2,64,2048]{3,2,1,0:T(8,128)(2,1)}, u32[]{:S(2)}) copy-start(bf16[2,2,64,2048]{3,2,1,0:T(8,128)(2,1)} %param.6) | copy-start | bytes 3145732
  169.4 1.6 copy-start
Sparse Core Ops, SparseCore 0:
  10.1 117.5 all-gather.2
  129.8 39.5 all-gather.4

commit v4 on v3

--- a/solution.py
+++ b/solution.py
@@ -108,17 +108,7 @@
     count = blocks * spins
     outer = count // ROWS
     first = pl.program_id(1) * ROWS
-    for j in range(ROWS):
-        for part in range(2):
-            start = first + j + part * detectors
-            for (first_k, size), spin_ref in zip(chunks, spin_refs):
-                for b in range(blocks):
-                    rows[j % 2, pl.ds(part * count + b * spins + first_k, size), :] = spin_ref[
-                        0, pl.ds(b * size * 2 * detectors + start, size, stride=2 * detectors), :
-                    ]
-        cycle = jnp.dot(
-            rows[j % 2].astype(jnp.bfloat16), phase_ref[j], preferred_element_type=jnp.float32
-        )
+    def add_pair(cycle, j):
         base_cos = orient_ref[j, :ROWS]
         base_sin = orient_ref[j, ROWS : 2 * ROWS]
         total = jnp.zeros((ROWS, samples), jnp.float32)
@@ -130,6 +120,38 @@
             total += oc * (real * base_cos - imag * base_sin)
             total -= os * (real * base_sin + imag * base_cos)
         out_ref[pl.ds(j, 1), :] = jnp.sum(total, axis=0, keepdims=True)
+
+    width = phase_ref.shape[1]
+    pairs_each = 2
+    for half in range(pairs_each):
+        other = (1 - half) * width
+        rows[:, pl.ds(half * 2 * count, 2 * count), pl.ds(other, width)] = jnp.zeros(
+            (2, 2 * count, width), jnp.float32
+        )
+    for j in range(ROWS):
+        half = j % pairs_each
+        slot = (j // pairs_each) % 2
+        base = half * 2 * count
+        for part in range(2):
+            start = first + j + part * detectors
+            for (first_k, size), spin_ref in zip(chunks, spin_refs):
+                for b in range(blocks):
+                    rows[
+                        slot,
+                        pl.ds(base + part * count + b * spins + first_k, size),
+                        pl.ds(half * width, width),
+                    ] = spin_ref[
+                        0, pl.ds(b * size * 2 * detectors + start, size, stride=2 * detectors), :
+                    ]
+        if half != pairs_each - 1:
+            continue
+        phases = phase_ref[j - 1 : j + 1].reshape(pairs_each * width, samples)
+        both = jnp.dot(
+            rows[slot].astype(jnp.bfloat16), phases, preferred_element_type=jnp.float32
+        )
+        for pair in range(pairs_each):
+            at = j - 1 + pair
+            add_pair(both[pair * 2 * count : (pair + 1) * 2 * count], at)
 
 
 def body(wigner, sky_blocks, beam, block_order, pointing):
@@ -237,7 +259,7 @@
         ],
         out_specs=pl.BlockSpec((ROWS, samples), row_of),
         out_shape=jax.ShapeDtypeStruct((pairs, samples), jnp.float32),
-        scratch_shapes=[pltpu.VMEM((2, 2 * blocks * spins, 2 * block_size), jnp.float32)],
+        scratch_shapes=[pltpu.VMEM((2, 4 * blocks * spins, 4 * block_size), jnp.float32)],
         compiler_params=params,
         cost_estimate=pl.CostEstimate(flops=2 * 10**10, bytes_accessed=5 * 10**7, transcendentals=0),
         name="stream",

time: 235 us -> 234 us (level)
  no operation moved by 1% of the time
where the time goes in v4:
time: 234 us; the launch traced here: 233 us
  Pallas kernels  111 us (47%)
  waiting for transfers between devices  57 us (24%)
  blocking collectives  44.1 us (19%)
  between operations  13.5 us (6%)
  local copies, waits for them, and re-layouts  5.72 us (2%)
    all_gather x2, waiting for transfers between devices, body(): whole = lax.all_gather(piece, 'sky', axis=0, tiled=True)  57 us
    pallas_call x2, Pallas kernels, body(): pl.pallas_call(functools.partial(spin_kernel, first_k), grid=(size,), in_...  42.1 us
    pallas_call x1, Pallas kernels, body(): pl.pallas_call(functools.partial(phase_kernel, cycle_pixels, orient_bins,...  37.4 us
    pallas_call x1, Pallas kernels, body(): pl.pallas_call(functools.partial(stream_kernel, chunks, detectors, blocks...  31.6 us
    all_gather x1, blocking collectives, body(): points = lax.all_gather(pointing, 'sky', axis=0, tiled=True)  26.4 us
    all_to_all x1, blocking collectives, body(): lax.all_to_all(stream.reshape(owners, pointing.shape[0], samples), 'sky',...  17.7 us
  transfers between devices with their start and end apart: 2, of which 2 were waited for; matrix products, arithmetic and copies ran while one was open for 1% of the time, Pallas kernels for 32%

profile of v4, /device:TPU:0, one launch (start us, length us, event | category | flops | bytes accessed | tf_op | source)
XLA Modules:
  0.0 233.4 jit_solution(3380954766016435497)
XLA Ops:
  6.5 0.0 all-gather.3.cloned.1.call-start
  6.6 1.6 copy.11
  8.2 0.1 broadcast_select_fusion
  8.3 1.7 copy.12
  9.9 0.0 all-gather.3.cloned.1.call-update
  9.9 0.0 all-gather.5.cloned.1.call-start
  10.0 0.1 slice.8
  10.1 0.7 broadcast_multiply_fusion
  10.8 26.4 %all_gather.9.pointing_ref = s32[128,1024]{1,0:T(8,128)S(1)} all-gather(s32[8,1024]{1,0:T(8,128)} %param.9), channel_id=1, replica_groups=mesh['groups'=2,'sky'=16] {'sky'}, dimensions={0}, use_global_device_ids=true | all-gather | bytes 557056 | tf_op jit(solution)/shard_map/all_gather | solution.py:176
  37.2 0.0 copy-start.1
  37.2 37.4 %phases.1 = (bf16[128,128,1024]{2,1,0:T(8,128)(2,1)}, f32[128,32,1024]{2,1,0:T(8,128)}) custom-call(s32[2]{0:T(128)S(1)} %get-tuple-element.20.order_ref, s32[128,1024]{1,0:T(8,128)S(1)} %all_gather.9.pointing_ref), custom_call_target="tpu_custom_call" | custom-call | flops 10000000000 | bytes 50000000 | tf_op jit(solution)/shard_map/phases/pallas_call | solution.py:183
  74.6 53.0 %all-gather.3.cloned.1.call-done = bf16[57344,128]{1,0:T(8,128)(2,1)} async-done(((bf16[3584,128]{1,0:T(8,128)(2,1)}), bf16[57344,128]{1,0:T(8,128)(2,1)}) %all-gather.3.cloned.1.call-update) | async-done | bytes 14680080 | tf_op jit(solution)/shard_map/all_gather | solution.py:209
  127.7 0.8 copy.13
  128.4 0.0 all-gather.5.cloned.1.call-update
  128.4 0.1 iota_add_fusion
  128.5 0.2 iota_compare_fusion
  128.7 0.0 copy-done.1
  128.8 0.1 broadcast_select_fusion.1.sky_ref
  128.9 36.6 %spin_0.1 = f32[2,2,28,128,128]{4,3,2,1,0:T(8,128)} custom-call(s32[2]{0:T(128)S(1)} %get-tuple-element.20.order_ref, bf16[2,2,32,64,2048]{4,3,2,1,0:T(8,128)(2,1)} %wigner_ref.3, bf16[2,2,64,2048]{3,2,1,0:T(8,128)(2,1)S(1)} %broadcast_select_fusion.1.sky_ref, bf16[16,28,128,128]{3,2,1,0:T(8,128)(2,1)} %bitcast.24), custom_call_target="tpu_custom_call" | custom-call | flops 28000000000 | bytes 56000000 | tf_op jit(solution)/shard_map/spin_0/pallas_call | solution.py:215
  165.5 3.9 %all-gather.5.cloned.1.call-done = bf16[8192,128]{1,0:T(8,128)(2,1)} async-done(((bf16[512,128]{1,0:T(8,128)(2,1)}), bf16[8192,128]{1,0:T(8,128)(2,1)}) %all-gather.5.cloned.1.call-update) | async-done | bytes 2097168 | tf_op jit(solution)/shard_map/all_gather | solution.py:209
  169.4 0.0 copy-start
  169.4 1.6 copy-done
  171.0 5.5 %spin_1.1 = f32[2,2,4,128,128]{4,3,2,1,0:T(8,128)S(1)} custom-call(s32[2]{0:T(128)S(1)} %get-tuple-element.20.order_ref, bf16[2,2,32,64,2048]{4,3,2,1,0:T(8,128)(2,1)} %wigner_ref.3, bf16[2,2,64,2048]{3,2,1,0:T(8,128)(2,1)S(1)} %broadcast_select_fusion.1.sky_ref, bf16[16,4,128,128]{3,2,1,0:T(8,128)(2,1)S(1)} %bitcast.16), custom_call_target="tpu_custom_call" | custom-call | flops 4000000000 | bytes 8000000 | tf_op jit(solution)/shard_map/spin_1/pallas_call | solution.py:215
  176.6 31.6 %stream.1 = f32[128,1024]{1,0:T(8,128)S(1)} custom-call(f32[2,7168,128]{2,1,0:T(8,128)} %bitcast.25, f32[2,1024,128]{2,1,0:T(8,128)S(1)} %bitcast.17, bf16[128,128,1024]{2,1,0:T(8,128)(2,1)} %get-tuple-element.17.refs_2_, f32[128,32,1024]{2,1,0:T(8,128)} %get-tuple-element.18.refs_3_), custom_call_target="tpu_custom_call" | custom-call | flops 20000000000 | bytes 50000000 | tf_op jit(solution)/shard_map/stream/pallas_call | solution.py:250
  208.1 17.7 %all_to_all.5 = f32[16,8,1024]{2,1,0:T(8,128)S(1)} all-to-all(f32[16,8,1024]{2,1,0:T(8,128)S(1)} %bitcast.18), channel_id=1, replica_groups=mesh['groups'=2,'sky'=16] {'sky'}, dimensions={0} | all-to-all | bytes 1048576 | tf_op jit(solution)/shard_map/all_to_all | solution.py:269
  225.9 0.6 reduce_sum.9
  (3 shorter events, 0.0 us)
Async XLA Ops:
  6.5 121.1 %all-gather.3.cloned.1.call-start = ((), (), s32[]{:S(2)}) async-start(), calls=%async_computation.1 | async-start | bytes 15597568 | tf_op jit(solution)/shard_map/all_gather | solution.py:209
  9.9 159.5 %all-gather.5.cloned.1.call-start = ((), (), s32[]{:S(2)}) async-start(), calls=%async_computation.2 | async-start | bytes 2228224 | tf_op jit(solution)/shard_map/all_gather | solution.py:209
  37.2 91.5 %copy-start.1 = (bf16[2,2,64,2048]{3,2,1,0:T(8,128)(2,1)S(1)}, bf16[2,2,64,2048]{3,2,1,0:T(8,128)(2,1)}, u32[]{:S(2)}) copy-start(bf16[2,2,64,2048]{3,2,1,0:T(8,128)(2,1)} %param.6) | copy-start | bytes 3145732
  169.4 1.6 copy-start
Sparse Core Ops, SparseCore 0:
  10.1 117.5 all-gather.2
  129.8 39.5 all-gather.4
